TPU v7x, 32 devices: a whole 2x2x4 slice. The times are simulated.
32 devices in a mesh: seq: 8 (over z, y), trk: 4 (over x, core).
Axes of the slice: x: 2, y: 2, z: 4, core: 2. Of those that a mesh axis runs over, the one named last changes fastest.
Arguments:
- bins: bfloat16 [8192, 768], P(('seq', 'trk')), may hold values from -6.7 to 6.7
- species: int32 [8], replicated, may hold values from 0 to 1, as said below
- cot_human: bfloat16 [8192, 5313], P(('seq', 'trk')), may hold values from -6.7 to 6.7
- cot_mouse: bfloat16 [8192, 1643], P(('seq', 'trk')), may hold values from -6.7 to 6.7
- norm_params: float32 [2304], P(('seq', 'trk')), may hold values from -1.6 to 1.6
- norm_first: float32 [2304], P(('seq', 'trk')), may hold values from -32 to 32
- norm_second: float32 [2304], P(('seq', 'trk')), may hold values from 2.048 to 8.192
- dilated_weight: float32 [3, 768, 384], P(None, ('seq', 'trk')), may hold values from -0.13958333 to 0.13958333
- dilated_first: float32 [3, 768, 384], P(None, ('seq', 'trk')), may hold values from -20.817224 to 20.817224
- dilated_second: float32 [3, 768, 384], P(None, ('seq', 'trk')), may hold values from 0.73728 to 2.94912
- point_weight: float32 [384, 768], P(None, ('seq', 'trk')), may hold values from -0.5460321 to 0.5460321
- point_first: float32 [384, 768], P(None, ('seq', 'trk')), may hold values from -20.817224 to 20.817224
- point_second: float32 [384, 768], P(None, ('seq', 'trk')), may hold values from 0.73728 to 2.94912
- final_weight: float32 [768, 1536], P(None, ('seq', 'trk')), may hold values from -0.40414519 to 0.40414519
- final_first: float32 [768, 1536], P(None, ('seq', 'trk')), may hold values from -33.48858 to 33.48858
- final_second: float32 [768, 1536], P(None, ('seq', 'trk')), may hold values from 0.73728 to 2.94912
- human_weight: float32 [1536, 5313], P(('seq', 'trk')), may hold values from -0.2857738 to 0.2857738
- human_first: float32 [1536, 5313], P(('seq', 'trk')), may hold values from -22.627417 to 22.627417
- human_second: float32 [1536, 5313], P(('seq', 'trk')), may hold values from 0.32768 to 1.31072
- mouse_weight: float32 [1536, 1643], P(('seq', 'trk')), may hold values from -0.2857738 to 0.2857738
- mouse_first: float32 [1536, 1643], P(('seq', 'trk')), may hold values from -22.627417 to 22.627417
- mouse_second: float32 [1536, 1643], P(('seq', 'trk')), may hold values from 0.32768 to 1.31072
Outputs:
- human_output: float32 [8192, 5313], P(('seq', 'trk'))
- mouse_output: float32 [8192, 1643], P(('seq', 'trk'))
- input_grad: float32 [8192, 768], P(('seq', 'trk'))
- norm_momentum: float32 [2304], P(('seq', 'trk'))
- norm_variance: float32 [2304], P(('seq', 'trk'))
- norm_updated: float32 [2304], P(('seq', 'trk'))
- dilated_momentum: float32 [3, 768, 384], P(None, ('seq', 'trk'))
- dilated_variance: float32 [3, 768, 384], P(None, ('seq', 'trk'))
- dilated_updated: float32 [3, 768, 384], P(None, ('seq', 'trk'))
- point_momentum: float32 [384, 768], P(None, ('seq', 'trk'))
- point_variance: float32 [384, 768], P(None, ('seq', 'trk'))
- point_updated: float32 [384, 768], P(None, ('seq', 'trk'))
- final_momentum: float32 [768, 1536], P(None, ('seq', 'trk'))
- final_variance: float32 [768, 1536], P(None, ('seq', 'trk'))
- final_updated: float32 [768, 1536], P(None, ('seq', 'trk'))
- human_momentum: float32 [1536, 5313], P(('seq', 'trk'))
- human_variance: float32 [1536, 5313], P(('seq', 'trk'))
- human_updated: float32 [1536, 5313], P(('seq', 'trk'))
- mouse_momentum: float32 [1536, 1643], P(('seq', 'trk'))
- mouse_variance: float32 [1536, 1643], P(('seq', 'trk'))
- mouse_updated: float32 [1536, 1643], P(('seq', 'trk'))
- trust_stats: float32 [3, 5], replicated
Inputs may be any that keep to these rules, and one draw needn't show every extreme that they name: Both species occur.
All inputs are finite; a program needn't handle non-finite values.
Results may differ from a plain program's by a relative error of at most 0.01.
The roundings to bfloat16 on the way count: a program that leaves them out, or rounds other values in their place, can miss the bound.
Values may be sent and summed in bfloat16 or wider, within the bound.
No kernel may reach another device: no remote copies, remote signals or barrier semaphores. Data moves between devices by JAX's collectives and lax.ppermute only.
A program may use at most 192 MiB of HBM per device.

v0:
```python
import jax
import jax.numpy as jnp
from jax import lax
from jax.sharding import PartitionSpec as P

C = 768
B = 384
DILATION_GAP = 57
WINDOW_BINS = 1024
STEP = 10


bn_eps = 1e-05
beta_first = 0.9
beta_second = 0.999
adam_eps = 1e-06
decay_rate = 0.01
matrix_rate = 0.5
norm_rate = 0.2


def extended(cells, sides, width):
    for axis, dim in sides:
        count = lax.axis_size(axis)
        ends = count - 1
        head = lax.slice_in_dim(cells, 0, width, axis=dim)
        tail = lax.slice_in_dim(cells, cells.shape[dim] - width, cells.shape[dim], axis=dim)
        cells = jnp.concatenate(
            [
                lax.ppermute(tail, axis, [(i, (i + 1) % count) for i in range(ends)]),
                cells,
                lax.ppermute(head, axis, [((i + 1) % count, i) for i in range(ends)]),
            ],
            axis=dim,
        )
    return cells


def gelu_back(inputs, gradient):
    unused, pullback = jax.vjp(jax.nn.gelu, inputs)
    return pullback(gradient)[0]


def contracted_rows(left, right):
    return lax.dot_general(
        left, right, (((0,), (0,)), ((), ())), preferred_element_type=jnp.float32
    )


def contract_cols(left, right):
    return lax.dot_general(
        left, right, (((1,), (1,)), ((), ())), preferred_element_type=jnp.float32
    )


def moments(momentum_old, variance_old, gradient):
    momentum = beta_first * momentum_old + (1.0 - beta_first) * gradient
    variance = beta_second * variance_old + (1.0 - beta_second) * gradient * gradient
    direction = (
        momentum
        / (1.0 - beta_first**STEP)
        / (jnp.sqrt(variance / (1.0 - beta_second**STEP)) + adam_eps)
    )
    return (momentum, variance, direction)


def body(
    bins,
    species,
    cot_human,
    cot_mouse,
    norm_params,
    norm_first,
    norm_second,
    dilated_weight,
    dilated_first,
    dilated_second,
    point_weight,
    point_first,
    point_second,
    final_weight,
    final_first,
    final_second,
    human_weight,
    human_first,
    human_second,
    mouse_weight,
    mouse_first,
    mouse_second,
):
    window_rows = bins.shape[0]
    seq_count = lax.axis_size("seq")
    trk_count = lax.axis_size("trk")
    total_rows = window_rows * seq_count * trk_count
    window_len = WINDOW_BINS
    first_row = lax.axis_index(("seq", "trk")) * window_rows
    window_id = first_row // window_len
    human_flag = lax.dynamic_index_in_dim(species, window_id, keepdims=False) == 0
    human_mask = human_flag.astype(jnp.float32)
    dilated_full, point_full, final_full, params_low = (
        lax.all_gather(dilated_weight.astype(jnp.bfloat16), ("seq", "trk"), axis=1, tiled=True),
        lax.all_gather(point_weight.astype(jnp.bfloat16), ("seq", "trk"), axis=1, tiled=True),
        lax.all_gather(final_weight.astype(jnp.bfloat16), ("seq", "trk"), axis=1, tiled=True),
        lax.all_gather(norm_params.astype(jnp.bfloat16), ("seq", "trk"), axis=0, tiled=True),
    )
    params = params_low.astype(jnp.float32)
    gain_one = params[:C]
    shift_one = params[C : 2 * C]
    gain_two = params[2 * C : 2 * C + B]
    shift_two = params[2 * C + B :]
    values = bins.astype(jnp.float32)
    one_stats = lax.psum((jnp.sum(values, 0), jnp.sum(values * values, 0)), ("seq", "trk"))
    mean_one = one_stats[0] / total_rows
    inverse_one = lax.rsqrt(one_stats[1] / total_rows - mean_one * mean_one + bn_eps)
    normed_one = (values - mean_one) * inverse_one
    affine_one = normed_one * gain_one + shift_one
    first_hidden = jax.nn.gelu(affine_one).astype(jnp.bfloat16)
    tap_positions = first_row - DILATION_GAP + jnp.arange(window_rows + 2 * DILATION_GAP)
    interior_slice = (jnp.floor_divide(tap_positions, window_len) == window_id).astype(
        jnp.bfloat16
    )[:, None]
    padded_input = extended(first_hidden, (("trk", 0),), DILATION_GAP) * interior_slice
    middle = jnp.zeros((window_rows, B), jnp.float32)
    for kernel_tap_index in range(3):
        middle = middle + jnp.dot(
            padded_input[
                kernel_tap_index * DILATION_GAP : kernel_tap_index * DILATION_GAP + window_rows
            ],
            dilated_full[kernel_tap_index],
            preferred_element_type=jnp.float32,
        )
    two_stats = lax.psum((jnp.sum(middle, 0), jnp.sum(middle * middle, 0)), ("seq", "trk"))
    mean_two = two_stats[0] / total_rows
    inverse_two = lax.rsqrt(two_stats[1] / total_rows - mean_two * mean_two + bn_eps)
    normed_two = (middle - mean_two) * inverse_two
    affine_two = normed_two * gain_two + shift_two
    hidden_two = jax.nn.gelu(affine_two).astype(jnp.bfloat16)
    residual = values + jnp.dot(hidden_two, point_full, preferred_element_type=jnp.float32)
    residual_low = residual.astype(jnp.bfloat16)
    lifted = jnp.dot(residual_low, final_full, preferred_element_type=jnp.float32)
    features = jax.nn.gelu(lifted).astype(jnp.bfloat16)
    human_cols = cot_human.shape[1]
    head_low = (human_weight.astype(jnp.bfloat16), mouse_weight.astype(jnp.bfloat16))
    pieces = (
        lax.all_gather(head_low[0], ("seq", "trk"), axis=0, tiled=True),
        lax.all_gather(head_low[1], ("seq", "trk"), axis=0, tiled=True),
    )
    columns = features
    human_logits = jnp.dot(columns, pieces[0], preferred_element_type=jnp.float32)
    mouse_logits = jnp.dot(columns, pieces[1], preferred_element_type=jnp.float32)
    human_output = jax.nn.softplus(human_logits) * human_mask
    mouse_output = jax.nn.softplus(mouse_logits) * (1.0 - human_mask)
    human_slope = (
        cot_human.astype(jnp.float32) * human_mask * jax.nn.sigmoid(human_logits)
    ).astype(jnp.bfloat16)
    mouse_slope = (
        cot_mouse.astype(jnp.float32) * (1.0 - human_mask) * jax.nn.sigmoid(mouse_logits)
    ).astype(jnp.bfloat16)
    joint_slope = jnp.concatenate([human_slope, mouse_slope], 1)
    pieces = (
        lax.all_gather(head_low[0], ("seq", "trk"), axis=0, tiled=True),
        lax.all_gather(head_low[1], ("seq", "trk"), axis=0, tiled=True),
    )
    part = contract_cols(human_slope, pieces[0]) + contract_cols(mouse_slope, pieces[1])
    columns = features
    head_sum = lax.psum_scatter(
        contracted_rows(columns, joint_slope), ("seq", "trk"), scatter_dimension=0, tiled=True
    )
    lifted_grad = gelu_back(lifted, part).astype(jnp.bfloat16)
    final_grad = contracted_rows(residual_low, lifted_grad)
    residual_grad = contract_cols(lifted_grad, final_full)
    branch_grad = residual_grad.astype(jnp.bfloat16)
    point_grad = contracted_rows(hidden_two, branch_grad)
    affine_two_grad = gelu_back(affine_two, contract_cols(branch_grad, point_full))
    two_back = lax.psum(
        (jnp.sum(affine_two_grad * normed_two, 0), jnp.sum(affine_two_grad, 0)), ("seq", "trk")
    )
    central_gradient = (
        gain_two
        * inverse_two
        * (affine_two_grad - two_back[1] / total_rows - normed_two * two_back[0] / total_rows)
    ).astype(jnp.bfloat16)
    padded_gradient = extended(central_gradient, (("trk", 0),), DILATION_GAP) * interior_slice
    hidden_one_grad = jnp.zeros((window_rows, C), jnp.float32)
    tap_grads = []
    for kernel_tap_index in range(3):
        tap_shift = (2 - kernel_tap_index) * DILATION_GAP
        hidden_one_grad = hidden_one_grad + contract_cols(
            padded_gradient[tap_shift : tap_shift + window_rows], dilated_full[kernel_tap_index]
        )
        tap_grads.append(
            contracted_rows(
                padded_input[
                    kernel_tap_index * DILATION_GAP : kernel_tap_index * DILATION_GAP + window_rows
                ],
                central_gradient,
            )
        )
    dilated_grad = jnp.stack(tap_grads)
    affine_one_grad = gelu_back(affine_one, hidden_one_grad)
    one_back = lax.psum(
        (jnp.sum(affine_one_grad * normed_one, 0), jnp.sum(affine_one_grad, 0)), ("seq", "trk")
    )
    input_grad = residual_grad + gain_one * inverse_one * (
        affine_one_grad - one_back[1] / total_rows - normed_one * one_back[0] / total_rows
    )
    norm_full = jnp.concatenate([one_back[0], one_back[1], two_back[0], two_back[1]])
    shard_len = norm_params.shape[0]
    norm_grad = lax.dynamic_slice_in_dim(
        norm_full, lax.axis_index(("seq", "trk")) * shard_len, shard_len
    )
    norm_momentum, norm_variance, norm_direction = moments(norm_first, norm_second, norm_grad)
    norm_updated = norm_params - norm_rate * norm_direction
    dilated_sum, point_sum, final_sum = (
        lax.psum_scatter(dilated_grad, ("seq", "trk"), scatter_dimension=1, tiled=True),
        lax.psum_scatter(point_grad, ("seq", "trk"), scatter_dimension=1, tiled=True),
        lax.psum_scatter(final_grad, ("seq", "trk"), scatter_dimension=1, tiled=True),
    )
    human_sum = head_sum[:, :human_cols]
    mouse_sum = head_sum[:, human_cols:]
    matrices = [
        (dilated_weight, dilated_first, dilated_second, dilated_sum),
        (point_weight, point_first, point_second, point_sum),
        (final_weight, final_first, final_second, final_sum),
        (human_weight, human_first, human_second, human_sum),
        (mouse_weight, mouse_first, mouse_second, mouse_sum),
    ]
    results = []
    weight_squares = []
    update_squares = []
    for kernel_weight, momentum_old, variance_old, gradient in matrices:
        momentum, variance, direction = moments(momentum_old, variance_old, gradient)
        update = direction + decay_rate * kernel_weight
        results.append((momentum, variance, update, kernel_weight))
        weight_squares.append(jnp.sum(kernel_weight * kernel_weight))
        update_squares.append(jnp.sum(update * update))
    square_sums = lax.psum(
        jnp.stack([jnp.stack(weight_squares), jnp.stack(update_squares)]), ("seq", "trk")
    )
    weight_norm = jnp.sqrt(square_sums[0])
    update_norm = jnp.sqrt(square_sums[1])
    ratio = weight_norm / (update_norm + adam_eps)
    updated = [
        results[index][3] - matrix_rate * ratio[index] * results[index][2] for index in range(5)
    ]
    trust_stats = jnp.stack([weight_norm, update_norm, ratio])
    return (
        human_output,
        mouse_output,
        input_grad,
        norm_momentum,
        norm_variance,
        norm_updated,
        results[0][0],
        results[0][1],
        updated[0],
        results[1][0],
        results[1][1],
        updated[1],
        results[2][0],
        results[2][1],
        updated[2],
        results[3][0],
        results[3][1],
        updated[3],
        results[4][0],
        results[4][1],
        updated[4],
        trust_stats,
    )


def solution(mesh):
    in_specs = (
        P(("seq", "trk"), None),
        P(),
        P(("seq", "trk"), None),
        P(("seq", "trk"), None),
        P(("seq", "trk")),
        P(("seq", "trk")),
        P(("seq", "trk")),
        P(None, ("seq", "trk"), None),
        P(None, ("seq", "trk"), None),
        P(None, ("seq", "trk"), None),
        P(None, ("seq", "trk")),
        P(None, ("seq", "trk")),
        P(None, ("seq", "trk")),
        P(None, ("seq", "trk")),
        P(None, ("seq", "trk")),
        P(None, ("seq", "trk")),
        P(("seq", "trk"), None),
        P(("seq", "trk"), None),
        P(("seq", "trk"), None),
        P(("seq", "trk"), None),
        P(("seq", "trk"), None),
        P(("seq", "trk"), None),
    )
    out_specs = (
        P(("seq", "trk"), None),
        P(("seq", "trk"), None),
        P(("seq", "trk"), None),
        P(("seq", "trk")),
        P(("seq", "trk")),
        P(("seq", "trk")),
        P(None, ("seq", "trk"), None),
        P(None, ("seq", "trk"), None),
        P(None, ("seq", "trk"), None),
        P(None, ("seq", "trk")),
        P(None, ("seq", "trk")),
        P(None, ("seq", "trk")),
        P(None, ("seq", "trk")),
        P(None, ("seq", "trk")),
        P(None, ("seq", "trk")),
        P(("seq", "trk"), None),
        P(("seq", "trk"), None),
        P(("seq", "trk"), None),
        P(("seq", "trk"), None),
        P(("seq", "trk"), None),
        P(("seq", "trk"), None),
        P(),
    )
    return jax.shard_map(body, mesh=mesh, in_specs=in_specs, out_specs=out_specs, check_vma=False)
```

profile of v0, /device:TPU:0, one launch (start us, length us, event | category | flops | bytes accessed | tf_op | source)
XLA Modules:
  0.0 1127.4 jit_solution(2850388290513096033)
XLA Ops:
  13.6 42.2 %all-reduce = bf16[2304]{0:T(1024)(128)(2,1)S(1)} all-reduce(bf16[2304]{0:T(1024)(128)(2,1)S(1)} %dynamic-update-slice), channel_id=1, replica_groups=mesh['seq'=8,'trk'=4] {'seq','trk'}, use_global_device_ids=true, to_apply=%add | all-reduce | flops 2304 | bytes 9216
  55.9 40.1 %all-reduce.5 = (f32[768]{0:T(1024)S(1)}, f32[768]{0:T(1024)S(1)}) all-reduce(f32[768]{0:T(1024)S(1)} %get-tuple-element.31, f32[768]{0:T(1024)S(1)} %get-tuple-element.30), channel_id=1, replica_groups=mesh['seq'=8,'trk'=4] {'seq','trk'}, use_global_device_ids=true, to_apply=%region_3.4 | all-reduce | flops 1536 | bytes 12288 | tf_op jit(solution)/shard_map/psum | solution.py:112
  100.4 46.4 %all_gather.22 = bf16[384,768]{0,1:T(8,128)(2,1)S(1)} all-gather(bf16[384,24]{0,1:T(8,128)(2,1)S(1)} %convert_element_type.77), channel_id=1, replica_groups=mesh['seq'=8,'trk'=4] {'seq','trk'}, dimensions={1}, use_global_device_ids=true | all-gather | bytes 608256 | tf_op jit(solution)/shard_map/all_gather | solution.py:102
  151.5 37.8 %all-reduce.4 = (f32[384]{0:T(512)S(1)}, f32[384]{0:T(512)S(1)}) all-reduce(f32[384]{0:T(512)S(1)} %get-tuple-element.29, f32[384]{0:T(512)S(1)} %get-tuple-element.28), channel_id=1, replica_groups=mesh['seq'=8,'trk'=4] {'seq','trk'}, use_global_device_ids=true, to_apply=%region_7.8 | all-reduce | flops 768 | bytes 6144 | tf_op jit(solution)/shard_map/psum | solution.py:132
  190.6 2.7 fusion.92
  193.2 5.9 all-gather.11.cloned.1.call-done
  199.1 7.3 multiply_convert_fusion.1
  207.4 2.8 fusion.93
  210.2 104.9 %all-gather.9.cloned.1.call-done = bf16[1536,5313]{1,0:T(8,128)(2,1)} async-done(((bf16[48,5313]{1,0:T(8,128)(2,1)}), bf16[1536,5313]{1,0:T(8,128)(2,1)}) %all-gather.9.cloned.1.call-update) | async-done | bytes 16321552 | tf_op jit(solution)/shard_map/all_gather | solution.py:145
  315.1 16.3 %multiply_convert_fusion = (bf16[256,5313]{0,1:T(8,128)(2,1)}, f32[256,5313]{0,1:T(8,128)}) fusion(bf16[256,5313]{0,1:T(8,128)(2,1)} %param.24, f32[]{:T(128)} %bitcast.3, bf16[1536,5313]{1,0:T(8,128)(2,1)} %all-gather.9.cloned.1.call-done, f32[256,1536]{1,0:T(8,128)S(1)} %fusion.92), kind=kOutput, calls=%fused_computation.2 | convolution fusion | flops 4200893952 | bytes 28775428 | tf_op jit(solution)/shard_map/dot_general | solution.py:149
  331.4 13.0 %fusion.12 = bf16[256,1536]{1,0:T(8,128)(2,1)} fusion(f32[256,1536]{1,0:T(8,128)S(1)} %fusion.92, f32[256,1536]{1,0:T(8,128)} %fusion.93, bf16[256,5313]{0,1:T(8,128)(2,1)} %get-tuple-element.62, bf16[1536,5313]{1,0:T(8,128)(2,1)} %all-gather.9.cloned.1.call-done), kind=kOutput, calls=%fused_computation.20 | convolution fusion | flops 4186570752 | bytes 22973952 | tf_op jit(solution)/shard_map/dot_general | solution.py:51
  344.4 2.7 fusion.94
  349.6 2.8 fusion.79
  352.4 38.4 %all-reduce.3 = (f32[384]{0:T(512)S(1)}, f32[384]{0:T(512)S(1)}) all-reduce(f32[384]{0:T(512)S(1)} %get-tuple-element.27, f32[384]{0:T(512)S(1)} %get-tuple-element.26), channel_id=1, replica_groups=mesh['seq'=8,'trk'=4] {'seq','trk'}, use_global_device_ids=true, to_apply=%region_11.12 | all-reduce | flops 768 | bytes 6144 | tf_op jit(solution)/shard_map/psum | solution.py:175
  393.2 2.0 pad_maximum_fusion
  396.3 4.2 fusion.95
  400.6 19.3 %fusion.1 = f32[1536,6956]{1,0:T(8,128)} fusion(bf16[256,1643]{0,1:T(8,128)(2,1)} %copy-done.17, bf16[256,5313]{0,1:T(8,128)(2,1)} %get-tuple-element.62, f32[256,1536]{1,0:T(8,128)S(1)} %fusion.92), kind=kOutput, calls=%fused_computation.4 | convolution fusion | flops 5481082880 | bytes 47872000 | tf_op jit(solution)/shard_map/dot_general | solution.py:45
  422.7 4.3 collective-permute-done.3
  428.1 2.4 fusion.78
  430.5 13.7 %reduce-scatter.13.cloned.1.call-done = f32[384,24]{0,1:T(8,128)} async-done(((f32[384,768]{0,1:T(8,128)}), f32[384,24]{0,1:T(8,128)}) %reduce-scatter.13.cloned.1.call-update) | async-done | bytes 36880
  444.2 2.1 multiply_reduce_fusion.11
  446.2 105.4 %reduce-scatter.7.cloned.1.call-done = f32[3,24,384]{2,1,0:T(8,128)} async-done(((f32[3,768,384]{2,1,0:T(8,128)}), f32[3,24,384]{2,1,0:T(8,128)}) %reduce-scatter.7.cloned.1.call-update) | async-done | bytes 110608 | tf_op jit(solution)/shard_map/reduce_scatter | solution.py:215
  551.7 2.4 multiply_reduce_fusion.9
  554.1 109.0 %reduce-scatter.9.cloned.1.call-done = f32[768,48]{0,1:T(8,128)} async-done(((f32[768,1536]{0,1:T(8,128)}), f32[768,48]{0,1:T(8,128)}) %reduce-scatter.9.cloned.1.call-update) | async-done | bytes 147472 | tf_op jit(solution)/shard_map/reduce_scatter | solution.py:217
  663.1 2.5 multiply_reduce_fusion.7
  665.7 387.7 %reduce-scatter.11.cloned.1.call-done = f32[48,6956]{1,0:T(8,128)} async-done(((f32[1536,6956]{1,0:T(8,128)}), f32[48,6956]{1,0:T(8,128)}) %reduce-scatter.11.cloned.1.call-update) | async-done | bytes 1335568 | tf_op jit(solution)/shard_map/reduce_scatter | solution.py:166
  1053.4 2.9 multiply_reduce_fusion.5
  1056.3 3.1 multiply_reduce_fusion.1
  1059.4 3.4 stack.72
  1062.8 3.3 stack.79
  1066.6 39.7 %all-reduce.2 = (f32[768]{0:T(1024)S(1)}, f32[768]{0:T(1024)S(1)}, f32[2,5]{1,0:T(2,128)}) all-reduce(f32[768]{0:T(1024)} %get-tuple-element.25, f32[768]{0:T(1024)} %get-tuple-element.24, f32[2,5]{1,0:T(2,128)} %pad_maximum_fusion.2), channel_id=1, replica_groups=mesh['seq'=8,'trk'=4] {'seq','trk'}, use_global_device_ids=true, to_apply=%region_15.16 | all-reduce | flops 1546 | bytes 12368 | tf_op jit(solution)/shard_map/psum | solution.py:201
  1113.0 2.6 fusion.35
  (131 shorter events, 35.1 us)
Async XLA Ops:
  7.2 5.2 copy-start
  7.2 139.9 %all-gather.5.cloned.1.call-start = ((), (), s32[]{:S(2)}) async-start(), calls=%async_computation.4 | async-start | bytes 1824768 | tf_op jit(solution)/shard_map/all_gather | solution.py:101
  8.9 46.9 %copy-start.3 = (bf16[256,768]{1,0:T(8,128)(2,1)S(1)}, bf16[256,768]{1,0:T(8,128)(2,1)}, u32[]{:S(2)}) copy-start(bf16[256,768]{1,0:T(8,128)(2,1)} %param.22) | copy-start | bytes 1179652
  8.9 181.7 %all-gather.7.cloned.1.call-start = ((), (), s32[]{:S(2)}) async-start(), calls=%async_computation.5 | async-start | bytes 2433024 | tf_op jit(solution)/shard_map/all_gather | solution.py:103
  10.6 188.6 %all-gather.11.cloned.1.call-start = ((), (), s32[]{:S(2)}) async-start(), calls=%async_computation.7 | async-start | bytes 5271552 | tf_op jit(solution)/shard_map/all_gather | solution.py:146
  12.3 86.8 %copy-start.30 = (s32[8]{0:T(128)S(1)}, s32[8]{0:T(128)}, u32[]{:S(2)}) copy-start(s32[8]{0:T(128)} %param.23) | copy-start | bytes 100
  12.3 88.1 %copy-start.23 = (f32[384,24]{0,1:T(8,128)S(1)}, f32[384,24]{0,1:T(8,128)}, u32[]{:S(2)}) copy-start(f32[384,24]{0,1:T(8,128)} %param.32) | copy-start | bytes 110596
  12.3 302.7 %all-gather.9.cloned.1.call-start = ((), (), s32[]{:S(2)}) async-start(), calls=%async_computation.6 | async-start | bytes 17031168 | tf_op jit(solution)/shard_map/all_gather | solution.py:145
  13.2 431.0 %reduce-scatter.13.cloned.1.call-start = ((), (), s32[]{:S(2)}) async-start(), calls=%async_computation.11 | async-start | bytes 1216512
  96.5 50.4 %collective-permute-start = (bf16[57,768]{1,0:T(8,128)(2,1)S(1)}, bf16[57,768]{1,0:T(8,128)(2,1)S(1)}, u32[]{:S(2)}, u32[]{:S(2)}) collective-permute-start(bf16[57,768]{1,0:T(8,128)(2,1)S(1)} %get-tuple-element.66), channel_id=1, source_target_pairs={{0,1},{1,2},{2,3},{4,5},{5,6},{6,7},{8,9},{9,10},{10,11},{12,13},{... | collective-permute-start | bytes 262664 | tf_op jit(solution)/shard_map/ppermute | solution.py:30
  97.8 49.1 %collective-permute-start.1 = (bf16[57,768]{1,0:T(8,128)(2,1)S(1)}, bf16[57,768]{1,0:T(8,128)(2,1)S(1)}, u32[]{:S(2)}, u32[]{:S(2)}) collective-permute-start(bf16[57,768]{1,0:T(8,128)(2,1)S(1)} %get-tuple-element.67), channel_id=1, source_target_pairs={{1,0},{2,1},{3,2},{5,4},{6,5},{7,6},{9,8},{10,9},{11,10},{13,12},{... | collective-permute-start | bytes 262664 | tf_op jit(solution)/shard_map/ppermute | solution.py:32
  146.9 42.5 %copy-start.18 = (bf16[384,768]{0,1:T(8,128)(2,1)}, bf16[384,768]{0,1:T(8,128)(2,1)S(1)}, u32[]{:S(2)}) copy-start(bf16[384,768]{0,1:T(8,128)(2,1)S(1)} %all_gather.22) | copy-start | bytes 1769476
  151.5 39.1 %copy-start.10 = (f32[256,384]{1,0:T(8,128)}, f32[256,384]{1,0:T(8,128)S(1)}, u32[]{:S(2)}) copy-start(f32[256,384]{1,0:T(8,128)S(1)} %get-tuple-element.88) | copy-start | bytes 1179652
  199.1 8.2 copy-start.29
  349.6 202.1 %reduce-scatter.7.cloned.1.call-start = ((), (), s32[]{:S(2)}) async-start(), calls=%async_computation.8 | async-start | bytes 3649536 | tf_op jit(solution)/shard_map/reduce_scatter | solution.py:215
  395.2 267.9 %reduce-scatter.9.cloned.1.call-start = ((), (), s32[]{:S(2)}) async-start(), calls=%async_computation.9 | async-start | bytes 4866048 | tf_op jit(solution)/shard_map/reduce_scatter | solution.py:217
  400.5 652.9 %reduce-scatter.11.cloned.1.call-start = ((), (), s32[]{:S(2)}) async-start(), calls=%async_computation.10 | async-start | bytes 44605440 | tf_op jit(solution)/shard_map/reduce_scatter | solution.py:166
  419.9 7.2 copy-start.9
  419.9 2.7 collective-permute-start.2
  421.4 5.6 collective-permute-start.3
  430.5 622.9 %copy-start.6 = (f32[48,1643]{1,0:T(8,128)S(1)}, f32[48,1643]{1,0:T(8,128)}, u32[]{:S(2)}) copy-start(f32[48,1643]{1,0:T(8,128)} %param.41) | copy-start | bytes 946372
  430.5 622.9 %copy-start.24 = (f32[48,1643]{1,0:T(8,128)S(1)}, f32[48,1643]{1,0:T(8,128)}, u32[]{:S(2)}) copy-start(f32[48,1643]{1,0:T(8,128)} %param.42) | copy-start | bytes 946372
  430.5 622.9 %copy-start.25 = (f32[48,1643]{1,0:T(8,128)S(1)}, f32[48,1643]{1,0:T(8,128)}, u32[]{:S(2)}) copy-start(f32[48,1643]{1,0:T(8,128)} %param.43) | copy-start | bytes 946372
  1059.4 59.2 %copy-start.1 = (f32[48,5313]{1,0:T(8,128)}, f32[48,5313]{1,0:T(8,128)S(1)}, u32[]{:S(2)}) copy-start(f32[48,5313]{1,0:T(8,128)S(1)} %get-tuple-element.54) | copy-start | bytes 3060292
  1059.4 59.2 %copy-start.2 = (f32[48,5313]{1,0:T(8,128)}, f32[48,5313]{1,0:T(8,128)S(1)}, u32[]{:S(2)}) copy-start(f32[48,5313]{1,0:T(8,128)S(1)} %get-tuple-element.55) | copy-start | bytes 3060292
  1106.4 9.2 copy-start.26
  1106.4 9.2 copy-start.27
  1106.4 9.8 copy-start.16
  1106.4 9.8 copy-start.21
  1106.4 9.8 copy-start.22
  1112.9 4.8 copy-start.7
  1112.9 4.8 copy-start.14
  (11 other events, 31.6 us)
Sparse Core Ops, SparseCore 0:
  11.5 58.5 all-gather.4
  73.6 56.2 all-gather.6
  133.3 65.7 all-gather.10
  202.5 112.5 all-gather.8
  349.7 94.4 reduce-scatter.12
  449.5 102.1 reduce-scatter.6
  557.1 105.9 reduce-scatter.8
  670.7 382.6 reduce-scatter.10
where the time goes:
time: 1130 us
  waiting for transfers between devices  731 us (65%)
  blocking collectives  245 us (22%)
  matrix products  82.6 us (7%)
  other arithmetic  33.2 us (3%)
  between operations  18.9 us (2%)
    reduce_scatter x1, waiting for transfers between devices, body(): lax.psum_scatter(contracted_rows(columns, joint_slope), ('seq', 'trk'), s...  388 us
    reduce_scatter x1, waiting for transfers between devices, body(): lax.psum_scatter(final_grad, ('seq', 'trk'), scatter_dimension=1, tiled=T...  109 us
    reduce_scatter x1, waiting for transfers between devices, body(): lax.psum_scatter(dilated_grad, ('seq', 'trk'), scatter_dimension=1, tiled...  105 us
    all_gather x1, waiting for transfers between devices, body(): lax.all_gather(head_low[0], ('seq', 'trk'), axis=0, tiled=True)  105 us
    all_gather x1, blocking collectives, body(): lax.all_gather(point_weight.astype(jnp.bfloat16), ('seq', 'trk'), axis=1,...  46.4 us
    unnamed x1, blocking collectives  42.2 us
    psum x1, blocking collectives, body(): lax.psum((jnp.sum(values, 0), jnp.sum(values * values, 0)), ('seq', 'trk'))  40.1 us
    psum x1, blocking collectives, body(): lax.psum((jnp.sum(affine_one_grad * normed_one, 0), jnp.sum(affine_one_gr...  39.7 us
  transfers between devices with their start and end apart: 12, of which 7 were waited for; matrix products, arithmetic and copies ran while one was open for 6% of the time, Pallas kernels for 0%

commit v1 on v0

--- a/solution.py
+++ b/solution.py
@@ -51,6 +51,13 @@
     return lax.dot_general(
         left, right, (((1,), (1,)), ((), ())), preferred_element_type=jnp.float32
     )
+
+
+def everywhere(vector):
+    axes = ("seq", "trk")
+    count = lax.axis_size("seq") * lax.axis_size("trk")
+    spread = jnp.broadcast_to(vector[None], (count,) + vector.shape)
+    return jnp.sum(lax.all_to_all(spread, axes, 0, 0, tiled=True), 0)
 
 
 def moments(momentum_old, variance_old, gradient):
@@ -97,19 +104,32 @@
     window_id = first_row // window_len
     human_flag = lax.dynamic_index_in_dim(species, window_id, keepdims=False) == 0
     human_mask = human_flag.astype(jnp.float32)
-    dilated_full, point_full, final_full, params_low = (
-        lax.all_gather(dilated_weight.astype(jnp.bfloat16), ("seq", "trk"), axis=1, tiled=True),
-        lax.all_gather(point_weight.astype(jnp.bfloat16), ("seq", "trk"), axis=1, tiled=True),
-        lax.all_gather(final_weight.astype(jnp.bfloat16), ("seq", "trk"), axis=1, tiled=True),
-        lax.all_gather(norm_params.astype(jnp.bfloat16), ("seq", "trk"), axis=0, tiled=True),
-    )
-    params = params_low.astype(jnp.float32)
+    devices = seq_count * trk_count
+    low = jnp.bfloat16
+    flat = jnp.concatenate(
+        [
+            dilated_weight.astype(low).reshape(-1),
+            point_weight.T.astype(low).reshape(-1),
+            final_weight.T.astype(low).reshape(-1),
+            jnp.pad(norm_params.astype(low), (0, -norm_params.shape[0] % 128)),
+        ]
+    )
+    trunk = lax.all_gather(flat.reshape(-1, 128), ("seq", "trk"), axis=0)
+    trunk = trunk.reshape(devices, -1)
+    ends = [dilated_weight.size, point_weight.size, final_weight.size]
+    ends = [ends[0], ends[0] + ends[1], ends[0] + ends[1] + ends[2]]
+    dilated_full = (
+        trunk[:, : ends[0]].reshape((devices,) + dilated_weight.shape).transpose(1, 0, 2, 3)
+    ).reshape(3, C, B)
+    point_full = trunk[:, ends[0] : ends[1]].reshape(C, B).T
+    final_full = trunk[:, ends[1] : ends[2]].reshape(-1, C).T
+    params = trunk[:, ends[2] : ends[2] + norm_params.shape[0]].reshape(-1).astype(jnp.float32)
     gain_one = params[:C]
     shift_one = params[C : 2 * C]
     gain_two = params[2 * C : 2 * C + B]
     shift_two = params[2 * C + B :]
     values = bins.astype(jnp.float32)
-    one_stats = lax.psum((jnp.sum(values, 0), jnp.sum(values * values, 0)), ("seq", "trk"))
+    one_stats = everywhere(jnp.stack([jnp.sum(values, 0), jnp.sum(values * values, 0)]))
     mean_one = one_stats[0] / total_rows
     inverse_one = lax.rsqrt(one_stats[1] / total_rows - mean_one * mean_one + bn_eps)
     normed_one = (values - mean_one) * inverse_one
@@ -129,7 +149,7 @@
             dilated_full[kernel_tap_index],
             preferred_element_type=jnp.float32,
         )
-    two_stats = lax.psum((jnp.sum(middle, 0), jnp.sum(middle * middle, 0)), ("seq", "trk"))
+    two_stats = everywhere(jnp.stack([jnp.sum(middle, 0), jnp.sum(middle * middle, 0)]))
     mean_two = two_stats[0] / total_rows
     inverse_two = lax.rsqrt(two_stats[1] / total_rows - mean_two * mean_two + bn_eps)
     normed_two = (middle - mean_two) * inverse_two
@@ -141,10 +161,10 @@
     features = jax.nn.gelu(lifted).astype(jnp.bfloat16)
     human_cols = cot_human.shape[1]
     head_low = (human_weight.astype(jnp.bfloat16), mouse_weight.astype(jnp.bfloat16))
-    pieces = (
-        lax.all_gather(head_low[0], ("seq", "trk"), axis=0, tiled=True),
-        lax.all_gather(head_low[1], ("seq", "trk"), axis=0, tiled=True),
-    )
+    human_pad = human_cols + -human_cols % 128
+    heads = jnp.concatenate([jnp.pad(head_low[0], ((0, 0), (0, human_pad - human_cols))), head_low[1]], 1)
+    heads = lax.all_gather(heads, ("seq", "trk"), axis=0, tiled=True)
+    pieces = (heads[:, :human_cols], heads[:, human_pad:])
     columns = features
     human_logits = jnp.dot(columns, pieces[0], preferred_element_type=jnp.float32)
     mouse_logits = jnp.dot(columns, pieces[1], preferred_element_type=jnp.float32)
@@ -156,15 +176,13 @@
     mouse_slope = (
         cot_mouse.astype(jnp.float32) * (1.0 - human_mask) * jax.nn.sigmoid(mouse_logits)
     ).astype(jnp.bfloat16)
-    joint_slope = jnp.concatenate([human_slope, mouse_slope], 1)
-    pieces = (
-        lax.all_gather(head_low[0], ("seq", "trk"), axis=0, tiled=True),
-        lax.all_gather(head_low[1], ("seq", "trk"), axis=0, tiled=True),
+    joint_slope = jnp.concatenate(
+        [jnp.pad(human_slope, ((0, 0), (0, human_pad - human_cols))), mouse_slope], 1
     )
     part = contract_cols(human_slope, pieces[0]) + contract_cols(mouse_slope, pieces[1])
     columns = features
     head_sum = lax.psum_scatter(
-        contracted_rows(columns, joint_slope), ("seq", "trk"), scatter_dimension=0, tiled=True
+        contracted_rows(columns, joint_slope).astype(low), ("seq", "trk"), scatter_dimension=0, tiled=True
     )
     lifted_grad = gelu_back(lifted, part).astype(jnp.bfloat16)
     final_grad = contracted_rows(residual_low, lifted_grad)
@@ -172,8 +190,8 @@
     branch_grad = residual_grad.astype(jnp.bfloat16)
     point_grad = contracted_rows(hidden_two, branch_grad)
     affine_two_grad = gelu_back(affine_two, contract_cols(branch_grad, point_full))
-    two_back = lax.psum(
-        (jnp.sum(affine_two_grad * normed_two, 0), jnp.sum(affine_two_grad, 0)), ("seq", "trk")
+    two_back = everywhere(
+        jnp.stack([jnp.sum(affine_two_grad * normed_two, 0), jnp.sum(affine_two_grad, 0)])
     )
     central_gradient = (
         gain_two
@@ -198,8 +216,8 @@
         )
     dilated_grad = jnp.stack(tap_grads)
     affine_one_grad = gelu_back(affine_one, hidden_one_grad)
-    one_back = lax.psum(
-        (jnp.sum(affine_one_grad * normed_one, 0), jnp.sum(affine_one_grad, 0)), ("seq", "trk")
+    one_back = everywhere(
+        jnp.stack([jnp.sum(affine_one_grad * normed_one, 0), jnp.sum(affine_one_grad, 0)])
     )
     input_grad = residual_grad + gain_one * inverse_one * (
         affine_one_grad - one_back[1] / total_rows - normed_one * one_back[0] / total_rows
@@ -211,13 +229,24 @@
     )
     norm_momentum, norm_variance, norm_direction = moments(norm_first, norm_second, norm_grad)
     norm_updated = norm_params - norm_rate * norm_direction
-    dilated_sum, point_sum, final_sum = (
-        lax.psum_scatter(dilated_grad, ("seq", "trk"), scatter_dimension=1, tiled=True),
-        lax.psum_scatter(point_grad, ("seq", "trk"), scatter_dimension=1, tiled=True),
-        lax.psum_scatter(final_grad, ("seq", "trk"), scatter_dimension=1, tiled=True),
-    )
+    flat_grads = jnp.concatenate(
+        [
+            dilated_grad.astype(low).reshape(3, devices, -1).transpose(1, 0, 2).reshape(devices, -1),
+            point_grad.astype(low).T.reshape(devices, -1),
+            final_grad.astype(low).T.reshape(devices, -1),
+        ],
+        1,
+    )
+    flat_sum = lax.psum_scatter(
+        flat_grads.reshape(devices, -1, 128), ("seq", "trk"), scatter_dimension=0, tiled=True
+    ).reshape(-1)
+    flat_sum = flat_sum.astype(jnp.float32)
+    dilated_sum = flat_sum[: ends[0]].reshape(dilated_weight.shape)
+    point_sum = flat_sum[ends[0] : ends[1]].reshape(point_weight.shape[::-1]).T
+    final_sum = flat_sum[ends[1] : ends[2]].reshape(final_weight.shape[::-1]).T
+    head_sum = head_sum.astype(jnp.float32)
     human_sum = head_sum[:, :human_cols]
-    mouse_sum = head_sum[:, human_cols:]
+    mouse_sum = head_sum[:, human_pad:]
     matrices = [
         (dilated_weight, dilated_first, dilated_second, dilated_sum),
         (point_weight, point_first, point_second, point_sum),
@@ -234,9 +263,7 @@
         results.append((momentum, variance, update, kernel_weight))
         weight_squares.append(jnp.sum(kernel_weight * kernel_weight))
         update_squares.append(jnp.sum(update * update))
-    square_sums = lax.psum(
-        jnp.stack([jnp.stack(weight_squares), jnp.stack(update_squares)]), ("seq", "trk")
-    )
+    square_sums = everywhere(jnp.stack([jnp.stack(weight_squares), jnp.stack(update_squares)]))
     weight_norm = jnp.sqrt(square_sums[0])
     update_norm = jnp.sqrt(square_sums[1])
     ratio = weight_norm / (update_norm + adam_eps)

time: 1130 us -> 688 us (0.61)
  waiting for transfers between devices: 731 us -> 471 us
  blocking collectives: 245 us -> 0 us
  local copies, waits for them, and re-layouts: 11.2 us -> 47.4 us
  starting transfers between devices: 5.68 us -> 36.4 us
  matrix products: 82.6 us -> 70.7 us
    reduce_scatter x3 -> x2, waiting for transfers between devices: 602 us -> 288 us  [the longest x1 221 us: body(): lax.psum_scatter(contracted_rows(columns, joint_slope).astype(low), ('seq...]
    psum x4 -> x0, blocking collectives: 156 us -> none  [the longest x1 40.1 us: body(): lax.psum((jnp.sum(values, 0), jnp.sum(values * values, 0)), ('seq', 'trk'))]
    all_gather x1 -> x0, blocking collectives: 46.4 us -> none  [body(): lax.all_gather(point_weight.astype(jnp.bfloat16), ('seq', 'trk'), axis=1,...]
    unnamed x1 -> x0, blocking collectives: 42.2 us -> none
    all_gather x4 -> x2, waiting for transfers between devices: 111 us -> 153 us  [the longest x1 105 us: body(): heads = lax.all_gather(heads, ('seq', 'trk'), axis=0, tiled=True)]
    all_to_all x0 -> x5, starting transfers between devices: none -> 28.8 us  [everywhere(): return jnp.sum(lax.all_to_all(spread, axes, 0, 0, tiled=True), 0)]
    all_to_all x0 -> x5, waiting for transfers between devices: none -> 26.6 us  [everywhere(): return jnp.sum(lax.all_to_all(spread, axes, 0, 0, tiled=True), 0)]
    unnamed x9 -> x4, waiting for transfers between devices: 13.8 us -> 0.07 us
  transfers between devices with their start and end apart: 12 -> 13, of which waited for: 7 -> 10; matrix products, arithmetic and copies ran while one was open for 6% -> 8% of each run, Pallas kernels for 0% -> 0%
where the time goes in v1:
time: 688 us; the launch traced here: 682 us
  waiting for transfers between devices  471 us (68%)
  matrix products  70.7 us (10%)
  local copies, waits for them, and re-layouts  47.4 us (7%)
  other arithmetic  38 us (6%)
  starting transfers between devices  36.4 us (5%)
  between operations  18.8 us (3%)
    reduce_scatter x1, waiting for transfers between devices, body(): lax.psum_scatter(contracted_rows(columns, joint_slope).astype(low), ('seq...  221 us
    all_gather x1, waiting for transfers between devices, body(): heads = lax.all_gather(heads, ('seq', 'trk'), axis=0, tiled=True)  105 us
    reduce_scatter x1, waiting for transfers between devices, body(): lax.psum_scatter(flat_grads.reshape(devices, -1, 128), ('seq', 'trk'), sc...  66.6 us
    all_gather x1, waiting for transfers between devices, body(): trunk = lax.all_gather(flat.reshape(-1, 128), ('seq', 'trk'), axis=0)  47.8 us
    all_to_all x5, starting transfers between devices, everywhere(): return jnp.sum(lax.all_to_all(spread, axes, 0, 0, tiled=True), 0)  28.8 us
    all_to_all x5, waiting for transfers between devices, everywhere(): return jnp.sum(lax.all_to_all(spread, axes, 0, 0, tiled=True), 0)  26.6 us
    dot_general x7, matrix products, contract_cols(): lax.dot_general(left, right, (((1,), (1,)), ((), ())), preferred_element_...  21.2 us
    dot_general x6, matrix products, contracted_rows(): lax.dot_general(left, right, (((0,), (0,)), ((), ())), preferred_element_...  18.9 us
  transfers between devices with their start and end apart: 13, of which 10 were waited for; matrix products, arithmetic and copies ran while one was open for 8% of the time, Pallas kernels for 0%

profile of v1, /device:TPU:0, one launch (start us, length us, event | category | flops | bytes accessed | tf_op | source)
XLA Modules:
  0.0 682.0 jit_solution(2403247700325325540)
XLA Ops:
  14.4 7.3 %all-to-all-start = ((f32[32,2,768]{2,1,0:T(2,128)}), f32[32,2,768]{2,1,0:T(2,128)S(1)}, u32[]{:S(2)}, u32[]{:S(2)}) async-start(f32[32,2,768]{2,1,0:T(2,128)} %broadcast_in_dim.10), calls=%async_computation | async-start | bytes 393216 | tf_op jit(solution)/shard_map/all_to_all | solution.py:60
  21.7 9.9 %all-to-all-done = f32[32,2,768]{2,1,0:T(2,128)S(1)} async-done(((f32[32,2,768]{2,1,0:T(2,128)}), f32[32,2,768]{2,1,0:T(2,128)S(1)}, u32[]{:S(2)}, u32[]{:S(2)}) %all-to-all-start) | async-done | bytes 196640 | tf_op jit(solution)/shard_map/all_to_all | solution.py:60
  31.8 47.8 %all-gather.3.cloned.1.call-done = bf16[32,577,128]{2,1,0:T(8,128)(2,1)} async-done(((bf16[1,577,128]{2,1,0:T(8,128)(2,1)}), bf16[32,577,128]{2,1,0:T(8,128)(2,1)}) %all-gather.3.cloned.1.call-update) | async-done | bytes 4726800 | tf_op jit(solution)/shard_map/all_gather | solution.py:117
  79.5 3.0 copy.94
  82.7 2.1 copy-done
  85.2 2.2 collective-permute-start
  94.0 8.2 %all-to-all-start.1 = ((f32[32,2,384]{2,1,0:T(2,128)}), f32[32,2,384]{2,1,0:T(2,128)S(1)}, u32[]{:S(2)}, u32[]{:S(2)}) async-start(f32[32,2,384]{2,1,0:T(2,128)} %broadcast_in_dim.11), calls=%async_computation.1 | async-start | bytes 196608 | tf_op jit(solution)/shard_map/all_to_all | solution.py:60
  104.7 3.3 slice.231
  109.0 3.0 reshape.209
  116.7 104.9 %all-gather.5.cloned.1.call-done = bf16[1536,7019]{1,0:T(8,128)(2,1)} async-done(((bf16[48,7019]{1,0:T(8,128)(2,1)}), bf16[1536,7019]{1,0:T(8,128)(2,1)}) %all-gather.5.cloned.1.call-update) | async-done | bytes 21562384 | tf_op jit(solution)/shard_map/all_gather | solution.py:166
  221.6 17.1 %multiply_convert_fusion = (bf16[256,5313]{0,1:T(8,128)(2,1)}, f32[256,5313]{0,1:T(8,128)}) fusion(bf16[256,5313]{0,1:T(8,128)(2,1)} %param.24, f32[]{:T(128)} %bitcast.7, bf16[1536,7019]{1,0:T(8,128)(2,1)} %all-gather.5.cloned.1.call-done, f32[256,1536]{1,0:T(8,128)} %fusion.117), kind=kOutput, calls=%fused_computation.9 | convolution fusion | flops 4200893952 | bytes 28973056 | tf_op jit(solution)/shard_map/dot_general | solution.py:169
  238.7 12.2 %fusion = f32[256,1536]{1,0:T(8,128)} fusion(bf16[256,5313]{0,1:T(8,128)(2,1)} %get-tuple-element.129, bf16[1536,7019]{1,0:T(8,128)(2,1)} %all-gather.5.cloned.1.call-done), kind=kOutput, calls=%fused_computation.2 | convolution fusion | flops 4178313216 | bytes 20811776 | tf_op jit(solution)/shard_map/dot_general | solution.py:51
  250.9 7.8 %multiply_convert_fusion.1 = (bf16[256,1643]{0,1:T(8,128)(2,1)S(1)}, f32[256,1643]{0,1:T(8,128)}) fusion(bf16[256,1643]{0,1:T(8,128)(2,1)} %param.25, f32[]{:T(128)S(6)} %sub.111, bf16[1536,7019]{1,0:T(8,128)(2,1)} %all-gather.5.cloned.1.call-done, f32[256,1536]{1,0:T(8,128)} %fusion.117), kind=kOutput, calls=%fused_computation.28 | convolution fusion | flops 1301535232 | bytes 10052100 | tf_op jit(solution)/shard_map/dot_general | solution.py:170
  258.7 5.3 fusion.26
  268.1 2.8 all-to-all-start.2
  272.2 2.1 convolution_convert_fusion.1
  274.3 2.5 reshape.212
  284.2 3.4 stack.133
  287.6 4.3 stack.131
  291.9 5.0 pad_maximum_fusion
  299.1 3.2 copy.92
  303.9 12.4 %convolution_convert_fusion = bf16[1536,7019]{1,0:T(8,128)(2,1)} fusion(bf16[256,5313]{0,1:T(8,128)(2,1)} %get-tuple-element.129, bf16[256,1643]{0,1:T(8,128)(2,1)S(1)} %copy-done.40, f32[256,1536]{1,0:T(8,128)S(1)} %copy-done.19), kind=kOutput, calls=%fused_computation | convolution fusion | flops 5545067520 | bytes 26696704 | tf_op jit(solution)/shard_map/dot_general | solution.py:45
  317.3 2.2 collective-permute-start.2
  325.6 6.4 all-to-all-start.3
  332.0 8.9 %all-to-all-done.3 = f32[32,2,768]{2,1,0:T(2,128)S(1)} async-done(((f32[32,2,768]{2,1,0:T(2,128)}), f32[32,2,768]{2,1,0:T(2,128)S(1)}, u32[]{:S(2)}, u32[]{:S(2)}) %all-to-all-start.3) | async-done | bytes 196640 | tf_op jit(solution)/shard_map/all_to_all | solution.py:60
  342.2 66.6 %reduce-scatter.3.cloned.1.call-done = bf16[1,576,128]{2,1,0:T(8,128)(2,1)} async-done(((bf16[32,576,128]{2,1,0:T(8,128)(2,1)}), bf16[1,576,128]{2,1,0:T(8,128)(2,1)}) %reduce-scatter.3.cloned.1.call-update) | async-done | bytes 147472 | tf_op jit(solution)/shard_map/reduce_scatter | solution.py:240
  412.7 2.4 multiply_reduce_fusion.9
  416.5 221.1 %reduce-scatter.5.cloned.1.call-done = bf16[48,7019]{1,0:T(8,128)(2,1)} async-done(((bf16[1536,7019]{1,0:T(8,128)(2,1)}), bf16[48,7019]{1,0:T(8,128)(2,1)}) %reduce-scatter.5.cloned.1.call-update) | async-done | bytes 673840 | tf_op jit(solution)/shard_map/reduce_scatter | solution.py:184
  642.5 3.4 stack.120
  645.9 3.4 stack.127
  649.9 4.1 all-to-all-start.4
  655.3 5.9 all-to-all-done.4
  (198 shorter events, 69.2 us)
Async XLA Ops:
  7.2 5.3 copy-start.2
  7.2 72.3 %all-gather.3.cloned.1.call-start = ((), (), s32[]{:S(2)}) async-start(), calls=%async_computation.7 | async-start | bytes 4933632 | tf_op jit(solution)/shard_map/all_gather | solution.py:117
  11.4 210.2 %all-gather.5.cloned.1.call-start = ((), (), s32[]{:S(2)}) async-start(), calls=%async_computation.8 | async-start | bytes 22302720 | tf_op jit(solution)/shard_map/all_gather | solution.py:166
  14.4 17.2 %all-to-all-start = ((f32[32,2,768]{2,1,0:T(2,128)}), f32[32,2,768]{2,1,0:T(2,128)S(1)}, u32[]{:S(2)}, u32[]{:S(2)}) async-start(f32[32,2,768]{2,1,0:T(2,128)} %broadcast_in_dim.10), calls=%async_computation | async-start | bytes 393216 | tf_op jit(solution)/shard_map/all_to_all | solution.py:60
  85.2 3.9 collective-permute-start
  87.4 3.8 collective-permute-start.1
  91.8 10.5 %copy-start.38 = (s32[8]{0:T(128)S(1)}, s32[8]{0:T(128)}, u32[]{:S(2)}) copy-start(s32[8]{0:T(128)} %param.23) | copy-start | bytes 100
  94.0 18.0 %all-to-all-start.1 = ((f32[32,2,384]{2,1,0:T(2,128)}), f32[32,2,384]{2,1,0:T(2,128)S(1)}, u32[]{:S(2)}, u32[]{:S(2)}) async-start(f32[32,2,384]{2,1,0:T(2,128)} %broadcast_in_dim.11), calls=%async_computation.1 | async-start | bytes 196608 | tf_op jit(solution)/shard_map/all_to_all | solution.py:60
  250.9 7.8 %copy-start.18 = (f32[256,1536]{1,0:T(8,128)S(1)}, f32[256,1536]{1,0:T(8,128)}, u32[]{:S(2)}) copy-start(f32[256,1536]{1,0:T(8,128)} %fusion.117) | copy-start | bytes 4718596
  250.9 7.8 %copy-start.41 = (f32[256,1536]{1,0:T(8,128)S(1)}, f32[256,1536]{1,0:T(8,128)}, u32[]{:S(2)}) copy-start(f32[256,1536]{1,0:T(8,128)} %fusion) | copy-start | bytes 4718596
  268.1 10.6 %all-to-all-start.2 = ((f32[32,2,384]{2,1,0:T(2,128)}), f32[32,2,384]{2,1,0:T(2,128)S(1)}, u32[]{:S(2)}, u32[]{:S(2)}) async-start(f32[32,2,384]{2,1,0:T(2,128)} %broadcast_in_dim.12), calls=%async_computation.2 | async-start | bytes 196608 | tf_op jit(solution)/shard_map/all_to_all | solution.py:60
  270.8 138.0 %reduce-scatter.3.cloned.1.call-start = ((), (), s32[]{:S(2)}) async-start(), calls=%async_computation.9 | async-start | bytes 4866048 | tf_op jit(solution)/shard_map/reduce_scatter | solution.py:240
  302.3 335.3 %reduce-scatter.5.cloned.1.call-start = ((), (), s32[]{:S(2)}) async-start(), calls=%async_computation.10 | async-start | bytes 22302720 | tf_op jit(solution)/shard_map/reduce_scatter | solution.py:184
  316.3 6.4 copy-start.16
  317.2 5.9 copy-start.4
  317.3 3.7 collective-permute-start.2
  319.4 3.1 collective-permute-start.3
  323.9 17.1 %copy-start.26 = (f32[256,768]{1,0:T(8,128)S(1)}, f32[256,768]{1,0:T(8,128)}, u32[]{:S(2)}) copy-start(f32[256,768]{1,0:T(8,128)} %copy-done.25) | copy-start | bytes 2359300
  325.6 15.3 %all-to-all-start.3 = ((f32[32,2,768]{2,1,0:T(2,128)}), f32[32,2,768]{2,1,0:T(2,128)S(1)}, u32[]{:S(2)}, u32[]{:S(2)}) async-start(f32[32,2,768]{2,1,0:T(2,128)} %broadcast_in_dim.13), calls=%async_computation.3 | async-start | bytes 393216 | tf_op jit(solution)/shard_map/all_to_all | solution.py:60
  341.0 70.3 %copy-start.31 = (f32[384,24]{0,1:T(8,128)S(1)}, f32[384,24]{0,1:T(8,128)}, u32[]{:S(2)}) copy-start(f32[384,24]{0,1:T(8,128)} %param.32) | copy-start | bytes 110596
  341.1 70.3 %copy-start.36 = (f32[384,24]{0,1:T(8,128)S(1)}, f32[384,24]{0,1:T(8,128)}, u32[]{:S(2)}) copy-start(f32[384,24]{0,1:T(8,128)} %param.33) | copy-start | bytes 110596
  341.1 70.3 %copy-start.37 = (f32[384,24]{0,1:T(8,128)S(1)}, f32[384,24]{0,1:T(8,128)}, u32[]{:S(2)}) copy-start(f32[384,24]{0,1:T(8,128)} %param.34) | copy-start | bytes 110596
  341.1 71.6 %copy-start.23 = (f32[3,24,384]{2,1,0:T(8,128)S(1)}, f32[3,24,384]{2,1,0:T(8,128)}, u32[]{:S(2)}) copy-start(f32[3,24,384]{2,1,0:T(8,128)} %param.29) | copy-start | bytes 331780
  341.1 74.0 %copy-start.20 = (f32[768,48]{0,1:T(8,128)S(1)}, f32[768,48]{0,1:T(8,128)}, u32[]{:S(2)}) copy-start(f32[768,48]{0,1:T(8,128)} %param.35) | copy-start | bytes 442372
  342.2 72.8 %copy-start.34 = (f32[768,48]{0,1:T(8,128)S(1)}, f32[768,48]{0,1:T(8,128)}, u32[]{:S(2)}) copy-start(f32[768,48]{0,1:T(8,128)} %param.36) | copy-start | bytes 442372
  342.2 72.8 %copy-start.35 = (f32[768,48]{0,1:T(8,128)S(1)}, f32[768,48]{0,1:T(8,128)}, u32[]{:S(2)}) copy-start(f32[768,48]{0,1:T(8,128)} %param.37) | copy-start | bytes 442372
  412.7 226.3 %copy-start.11 = (f32[48,1643]{1,0:T(8,128)S(1)}, f32[48,1643]{1,0:T(8,128)}, u32[]{:S(2)}) copy-start(f32[48,1643]{1,0:T(8,128)} %param.41) | copy-start | bytes 946372
  412.7 226.3 %copy-start.32 = (f32[48,1643]{1,0:T(8,128)S(1)}, f32[48,1643]{1,0:T(8,128)}, u32[]{:S(2)}) copy-start(f32[48,1643]{1,0:T(8,128)} %param.42) | copy-start | bytes 946372
  412.7 226.3 %copy-start.33 = (f32[48,1643]{1,0:T(8,128)S(1)}, f32[48,1643]{1,0:T(8,128)}, u32[]{:S(2)}) copy-start(f32[48,1643]{1,0:T(8,128)} %param.43) | copy-start | bytes 946372
  642.5 32.6 %copy-start.5 = (f32[48,5313]{1,0:T(8,128)}, f32[48,5313]{1,0:T(8,128)S(1)}, u32[]{:S(2)}) copy-start(f32[48,5313]{1,0:T(8,128)S(1)} %get-tuple-element.118) | copy-start | bytes 3060292
  642.5 32.6 %copy-start.6 = (f32[48,5313]{1,0:T(8,128)}, f32[48,5313]{1,0:T(8,128)S(1)}, u32[]{:S(2)}) copy-start(f32[48,5313]{1,0:T(8,128)S(1)} %get-tuple-element.119) | copy-start | bytes 3060292
  649.9 11.3 %all-to-all-start.4 = ((f32[32,2,5]{2,1,0:T(2,128)}), f32[32,2,5]{2,1,0:T(2,128)}, u32[]{:S(2)}, u32[]{:S(2)}) async-start(f32[32,2,5]{2,1,0:T(2,128)} %broadcast_in_dim.14), calls=%async_computation.6 | async-start | bytes 65536 | tf_op jit(solution)/shard_map/all_to_all | solution.py:60
  (23 other events, 49.1 us)
Sparse Core Ops, SparseCore 0:
  11.6 67.9 all-gather.2
  83.0 138.5 all-gather.4
  302.4 106.3 reduce-scatter.2
  416.2 221.3 reduce-scatter.4

commit v2 on v1

--- a/solution.py
+++ b/solution.py
@@ -1,6 +1,10 @@
+import functools
+
 import jax
 import jax.numpy as jnp
 from jax import lax
+from jax.experimental import pallas as pl
+from jax.experimental.pallas import tpu as pltpu
 from jax.sharding import PartitionSpec as P
 
 C = 768
@@ -58,6 +62,256 @@
     count = lax.axis_size("seq") * lax.axis_size("trk")
     spread = jnp.broadcast_to(vector[None], (count,) + vector.shape)
     return jnp.sum(lax.all_to_all(spread, axes, 0, 0, tiled=True), 0)
+
+
+def partner(cells, axis, mask):
+    return lax.ppermute(cells, axis, [(i, i ^ mask) for i in range(lax.axis_size(axis))])
+
+
+def digits(count):
+    found = [(0, 2)]
+    shift = 1
+    while 1 << shift < count:
+        radix = 4 if count >> shift >= 4 else 2
+        found.append((shift, radix))
+        shift += radix // 2
+    return found
+
+
+def turned(parts, digit):
+    bit = 1
+    while bit < len(parts):
+        flag = digit & bit != 0
+        parts = [jnp.where(flag, parts[r ^ bit], parts[r]) for r in range(len(parts))]
+        bit *= 2
+    return parts
+
+
+def collected(block):
+    cells = block[None]
+    steps = [("seq", shift, radix) for shift, radix in reversed(digits(lax.axis_size("seq")))]
+    steps += [("trk", shift, radix) for shift, radix in reversed(digits(lax.axis_size("trk")))]
+    for axis, shift, radix in steps:
+        parts = [cells] + [partner(cells, axis, r << shift) for r in range(1, radix)]
+        parts = turned(parts, lax.axis_index(axis) >> shift)
+        cells = jnp.stack(parts, 1).reshape((-1,) + block.shape)
+    return cells
+
+
+def summed_digits(total, steps):
+    for shift, radix in steps:
+        parts = total.reshape((radix, -1) + total.shape[1:])
+        total = parts[0]
+        sent = [parts[r].astype(jnp.bfloat16) for r in range(1, radix)]
+        for r in range(1, radix):
+            total = total + partner(sent[r - 1], "seq", r << shift).astype(jnp.float32)
+    return total
+
+
+def relative(cells, axis, digit):
+    parts = [lax.index_in_dim(cells, r, axis, keepdims=False) for r in range(cells.shape[axis])]
+    return jnp.stack(turned(parts, digit), axis)
+
+
+def halved(cells, at, axis, shift):
+    digit = lax.axis_index(axis) >> shift & 1
+    pick = lambda r: lax.dynamic_index_in_dim(cells, digit ^ r, at, keepdims=False)
+    got = partner(pick(1).astype(jnp.bfloat16), axis, 1 << shift)
+    return pick(0).astype(jnp.float32) + got.astype(jnp.float32)
+
+
+def scattered_near(cells):
+    shape = cells.shape[1:]
+    cut = shape[0] // 2
+    cells = halved(cells.reshape((-1, 2, 2, 2) + shape), 3, "trk", 0)
+    first, second = cells[:, :, :, :cut], cells[:, :, :, cut:]
+    first = halved(first, 2, "trk", 1)
+    second = halved(second, 1, "seq", 0)
+    first = halved(first, 1, "seq", 0)
+    second = halved(second, 1, "trk", 1)
+    return jnp.concatenate([first, second], 1)
+
+
+def scattered_far(cells):
+    steps = digits(lax.axis_size("seq"))[1:]
+    shape = cells.shape[1:]
+    cells = cells.reshape(tuple(radix for _, radix in reversed(steps)) + shape)
+    for place, (shift, radix) in enumerate(steps):
+        cells = relative(cells, len(steps) - 1 - place, lax.axis_index("seq") >> shift)
+    cells = cells.transpose(tuple(range(len(steps) - 1, -1, -1)) + (len(steps), len(steps) + 1))
+    return summed_digits(cells.reshape((-1,) + shape[1:]), steps)
+
+
+def relative_rows(features):
+    steps = digits(lax.axis_size("seq"))[1:]
+    columns = features.shape[1]
+    count = len(steps)
+    cells = features.reshape(tuple(radix for _, radix in reversed(steps)) + (2, 2, -1, columns))
+    for place, (shift, radix) in enumerate(steps):
+        cells = relative(cells, count - 1 - place, lax.axis_index("seq") >> shift)
+    higher = tuple(range(count - 1, -1, -1))
+    along_y = relative(cells, count, lax.axis_index("seq") & 1)
+    along_x = relative(cells, count + 1, lax.axis_index("trk") >> 1)
+    along_y = along_y.transpose((count,) + higher + (count + 1, count + 2, count + 3))
+    along_x = along_x.transpose((count + 1,) + higher + (count, count + 2, count + 3))
+    return along_y.reshape(-1, columns), along_x.reshape(-1, columns)
+
+
+def after(cells, other):
+    return cells + (other[(slice(0, 1),) * other.ndim].reshape((1,) * cells.ndim) * 0).astype(cells.dtype)
+
+
+def sides():
+    core = lax.axis_index("trk") & 1
+    x_place = lax.axis_index("trk")
+    y_place = (lax.axis_index("seq") & 1) * 2 + core
+    return (("trk", 2, x_place), ("seq", 1, y_place))
+
+
+def group_features(along_y, along_x):
+    pairs = [(along_y, partner(along_y, "trk", 2)), (along_x, partner(along_x, "seq", 1))]
+    return [
+        jnp.concatenate([own, got, partner(own, "trk", 1), partner(got, "trk", 1)], 1)
+        for own, got in pairs
+    ]
+
+
+def group_columns(slopes):
+    kept, given = [], []
+    for cells, (axis, mask, place) in zip(slopes, sides()):
+        pick = lambda r: lax.dynamic_index_in_dim(cells, place ^ r, 1, keepdims=False)
+        got = partner(jnp.stack([pick(2), pick(3)]), axis, mask)
+        kept.append(jnp.concatenate([pick(0), got[0]], 2))
+        given.append(jnp.concatenate([pick(1), got[1]], 2))
+    got = partner(jnp.stack(given), "trk", 1)
+    return [jnp.concatenate([kept[k], got[k]], 2) for k in range(2)]
+
+
+def product(left, right):
+    return lax.dot_general(left, right, (((1,), (1,)), ((), ())), preferred_element_type=jnp.float32)
+
+
+def halved_products(features, columns, part):
+    totals = []
+    for left, right, (axis, mask, place) in zip(features, columns, sides()):
+        cut = left.shape[0] // 2
+        other_axis, other_mask = ("seq", 1) if axis == "trk" else ("trk", 2)
+        got = partner(product(left[cut:], right[part]).astype(jnp.bfloat16), other_axis, other_mask)
+        totals.append(product(left[:cut], right[part]) + got.astype(jnp.float32))
+    return jnp.concatenate(totals, 1)
+
+
+def own_rows(total):
+    columns = total.shape[1] // 2
+    kept, given = [], []
+    for index, (axis, mask, place) in enumerate(sides()):
+        cells = total[:, index * columns : (index + 1) * columns].reshape(2, 2, -1, columns)
+        digit, core = place >> 1, place & 1
+        pick = lambda r: lax.dynamic_index_in_dim(cells, digit ^ r, 0, keepdims=False)
+        got = partner(pick(1), axis, mask)
+        pair = jnp.stack([jnp.where(digit == 0, pick(0), got), jnp.where(digit == 0, got, pick(0))], 1)
+        kept.append(lax.dynamic_index_in_dim(pair, core, 0, keepdims=False))
+        given.append(lax.dynamic_index_in_dim(pair, core ^ 1, 0, keepdims=False))
+    got = partner(jnp.stack(given), "trk", 1)
+    results = []
+    for index, (axis, mask, place) in enumerate(sides()):
+        core = place & 1
+        parts = [
+            jnp.where(core == 0, kept[index], got[index]),
+            jnp.where(core == 0, got[index], kept[index]),
+        ]
+        cells = jnp.stack(parts, 1).transpose(2, 0, 1, 3)
+        results.append(cells.reshape(cells.shape[0], 4 * columns).astype(jnp.float32))
+    return results
+
+
+def head_kernel(
+    human_cols, flag, features, weights, cot_human, cot_mouse, human, mouse, slopes, total
+):
+    step = pl.program_id(0)
+    chunk = slopes.shape[0]
+    sub = 256
+
+    @pl.when(step == 0)
+    def _():
+        total[...] = jnp.zeros_like(total)
+
+    def run(cots, out, first, width):
+        parts = []
+        for at in range(0, chunk, sub):
+            rows = max(min(sub, out.shape[0] - at), 0)
+            logits = jnp.dot(
+                features[...], weights[:, at : at + sub], preferred_element_type=jnp.float32
+            ).T
+            small = jnp.exp(-jnp.abs(logits))
+            sigmoid = jnp.where(logits >= 0, 1.0, small) / (1.0 + small)
+            positive = jnp.maximum(logits, 0.0) + jnp.log1p(small)
+            slope = jnp.zeros_like(logits)
+            if rows:
+                out[at : at + rows, :] = positive[:rows]
+                slope = cots[at : at + rows, :].astype(jnp.float32) * sigmoid[:rows]
+            if rows and rows < sub:
+                slope = jnp.concatenate([slope, jnp.zeros((sub - rows, slope.shape[1]), jnp.float32)])
+            column = first + at + lax.broadcasted_iota(jnp.int32, slope.shape, 0)
+            slope = jnp.where(column < width, slope, 0.0).astype(jnp.bfloat16)
+            slopes[at : at + sub, :] = slope
+            parts.append(slope)
+        total[...] += jnp.dot(
+            weights[...], jnp.concatenate(parts, 0), preferred_element_type=jnp.float32
+        )
+
+    @pl.when((step < 3) & (flag[0] != 0))
+    def _():
+        run(cot_human, human, step * chunk, human_cols)
+
+    @pl.when((step == 3) & (flag[0] == 0))
+    def _():
+        run(cot_mouse, mouse, 0, cot_mouse.shape[0])
+
+    @pl.when((step < 3) & (flag[0] == 0))
+    def _():
+        human[...] = jnp.zeros_like(human)
+        slopes[...] = jnp.zeros_like(slopes)
+
+    @pl.when((step == 3) & (flag[0] != 0))
+    def _():
+        mouse[...] = jnp.zeros_like(mouse)
+        slopes[...] = jnp.zeros_like(slopes)
+
+
+def heads_part(flag, features, heads, cot_human, cot_mouse, chunk):
+    rows, depth = features.shape
+    human_cols, mouse_cols = cot_human.shape[0], cot_mouse.shape[0]
+    return pl.pallas_call(
+        functools.partial(head_kernel, human_cols),
+        grid_spec=pltpu.PrefetchScalarGridSpec(
+            num_scalar_prefetch=1,
+            grid=(4,),
+            in_specs=[
+                pl.BlockSpec((rows, depth), lambda i, flag: (0, 0)),
+                pl.BlockSpec(
+                    (depth, chunk), lambda i, flag: (0, jnp.where(flag[0] != 0, jnp.minimum(i, 2), 3))
+                ),
+                pl.BlockSpec(
+                    (chunk, rows), lambda i, flag: (jnp.where(flag[0] != 0, jnp.minimum(i, 2), 0), 0)
+                ),
+                pl.BlockSpec((mouse_cols, rows), lambda i, flag: (0, 0)),
+            ],
+            out_specs=[
+                pl.BlockSpec((chunk, rows), lambda i, flag: (jnp.minimum(i, 2), 0)),
+                pl.BlockSpec((mouse_cols, rows), lambda i, flag: (0, 0)),
+                pl.BlockSpec((chunk, rows), lambda i, flag: (i, 0)),
+                pl.BlockSpec((depth, rows), lambda i, flag: (0, 0)),
+            ],
+        ),
+        out_shape=[
+            jax.ShapeDtypeStruct((human_cols, rows), jnp.float32),
+            jax.ShapeDtypeStruct((mouse_cols, rows), jnp.float32),
+            jax.ShapeDtypeStruct((4 * chunk, rows), jnp.bfloat16),
+            jax.ShapeDtypeStruct((depth, rows), jnp.float32),
+        ],
+        compiler_params=pltpu.CompilerParams(vmem_limit_bytes=48 * 2**20),
+    )(flag, features, heads, cot_human, cot_mouse)
 
 
 def moments(momentum_old, variance_old, gradient):
@@ -103,27 +357,34 @@
     first_row = lax.axis_index(("seq", "trk")) * window_rows
     window_id = first_row // window_len
     human_flag = lax.dynamic_index_in_dim(species, window_id, keepdims=False) == 0
-    human_mask = human_flag.astype(jnp.float32)
     devices = seq_count * trk_count
     low = jnp.bfloat16
-    flat = jnp.concatenate(
+    human_cols = cot_human.shape[1]
+    mouse_cols = cot_mouse.shape[1]
+    chunk = -(-human_cols // 768) * 256
+    heads = jnp.concatenate(
         [
-            dilated_weight.astype(low).reshape(-1),
-            point_weight.T.astype(low).reshape(-1),
-            final_weight.T.astype(low).reshape(-1),
-            jnp.pad(norm_params.astype(low), (0, -norm_params.shape[0] % 128)),
-        ]
-    )
-    trunk = lax.all_gather(flat.reshape(-1, 128), ("seq", "trk"), axis=0)
-    trunk = trunk.reshape(devices, -1)
-    ends = [dilated_weight.size, point_weight.size, final_weight.size]
-    ends = [ends[0], ends[0] + ends[1], ends[0] + ends[1] + ends[2]]
-    dilated_full = (
-        trunk[:, : ends[0]].reshape((devices,) + dilated_weight.shape).transpose(1, 0, 2, 3)
-    ).reshape(3, C, B)
-    point_full = trunk[:, ends[0] : ends[1]].reshape(C, B).T
-    final_full = trunk[:, ends[1] : ends[2]].reshape(-1, C).T
-    params = trunk[:, ends[2] : ends[2] + norm_params.shape[0]].reshape(-1).astype(jnp.float32)
+            jnp.pad(human_weight.astype(low), ((0, 0), (0, 3 * chunk - human_cols))),
+            jnp.pad(mouse_weight.astype(low), ((0, 0), (0, chunk - mouse_cols))),
+        ],
+        1,
+    )
+    heads = lax.all_gather(heads, ("seq", "trk"), axis=0, tiled=True)
+    own = dilated_weight.shape[1]
+    low_params = norm_params.astype(low)
+    low_params = jnp.pad(low_params, (0, 8 * B - low_params.shape[0])).reshape(8, B)
+    early = jnp.concatenate([dilated_weight.astype(low).reshape(-1, B), low_params])
+    final_low = final_weight.T.astype(low)
+    late = jnp.concatenate([point_weight.T.astype(low), final_low[:, :B], final_low[:, B:]])
+    early = collected(early)
+    late = collected(late)
+    dilated_full = early[:, : 3 * own].reshape(devices, 3, own, B).transpose(1, 0, 2, 3)
+    dilated_full = dilated_full.reshape(3, C, B)
+    params = early[:, 3 * own, : norm_params.shape[0]].reshape(-1).astype(jnp.float32)
+    point_full = late[:, :own].reshape(C, B)
+    final_full = jnp.concatenate(
+        [late[:, own : 3 * own].reshape(-1, B), late[:, 3 * own :].reshape(-1, B)], 1
+    )
     gain_one = params[:C]
     shift_one = params[C : 2 * C]
     gain_two = params[2 * C : 2 * C + B]
@@ -155,41 +416,29 @@
     normed_two = (middle - mean_two) * inverse_two
     affine_two = normed_two * gain_two + shift_two
     hidden_two = jax.nn.gelu(affine_two).astype(jnp.bfloat16)
-    residual = values + jnp.dot(hidden_two, point_full, preferred_element_type=jnp.float32)
+    residual = values + contract_cols(hidden_two, point_full)
     residual_low = residual.astype(jnp.bfloat16)
-    lifted = jnp.dot(residual_low, final_full, preferred_element_type=jnp.float32)
+    lifted = contract_cols(residual_low, final_full)
     features = jax.nn.gelu(lifted).astype(jnp.bfloat16)
-    human_cols = cot_human.shape[1]
-    head_low = (human_weight.astype(jnp.bfloat16), mouse_weight.astype(jnp.bfloat16))
-    human_pad = human_cols + -human_cols % 128
-    heads = jnp.concatenate([jnp.pad(head_low[0], ((0, 0), (0, human_pad - human_cols))), head_low[1]], 1)
-    heads = lax.all_gather(heads, ("seq", "trk"), axis=0, tiled=True)
-    pieces = (heads[:, :human_cols], heads[:, human_pad:])
-    columns = features
-    human_logits = jnp.dot(columns, pieces[0], preferred_element_type=jnp.float32)
-    mouse_logits = jnp.dot(columns, pieces[1], preferred_element_type=jnp.float32)
-    human_output = jax.nn.softplus(human_logits) * human_mask
-    mouse_output = jax.nn.softplus(mouse_logits) * (1.0 - human_mask)
-    human_slope = (
-        cot_human.astype(jnp.float32) * human_mask * jax.nn.sigmoid(human_logits)
-    ).astype(jnp.bfloat16)
-    mouse_slope = (
-        cot_mouse.astype(jnp.float32) * (1.0 - human_mask) * jax.nn.sigmoid(mouse_logits)
-    ).astype(jnp.bfloat16)
-    joint_slope = jnp.concatenate(
-        [jnp.pad(human_slope, ((0, 0), (0, human_pad - human_cols))), mouse_slope], 1
-    )
-    part = contract_cols(human_slope, pieces[0]) + contract_cols(mouse_slope, pieces[1])
-    columns = features
-    head_sum = lax.psum_scatter(
-        contracted_rows(columns, joint_slope).astype(low), ("seq", "trk"), scatter_dimension=0, tiled=True
-    )
+    rows_features = group_features(*relative_rows(features.T))
+    human_out, mouse_out, slopes, part = heads_part(
+        human_flag.astype(jnp.int32).reshape(1), features, heads, cot_human.T, cot_mouse.T, chunk
+    )
+    slopes = slopes.reshape(2, 2, 4, chunk // 4, window_rows)
+    columns = group_columns((slopes[:, 0], slopes[:, 1]))
+    early_total = halved_products(rows_features, columns, 0)
+    late_total = halved_products(rows_features, columns, 1)
+    human_output = human_out.T
+    mouse_output = mouse_out.T
+    part = part.T
     lifted_grad = gelu_back(lifted, part).astype(jnp.bfloat16)
-    final_grad = contracted_rows(residual_low, lifted_grad)
-    residual_grad = contract_cols(lifted_grad, final_full)
+    final_grad = contracted_rows(lifted_grad, residual_low)
+    residual_grad = jnp.dot(lifted_grad, final_full, preferred_element_type=jnp.float32)
     branch_grad = residual_grad.astype(jnp.bfloat16)
-    point_grad = contracted_rows(hidden_two, branch_grad)
-    affine_two_grad = gelu_back(affine_two, contract_cols(branch_grad, point_full))
+    point_grad = contracted_rows(branch_grad, hidden_two)
+    affine_two_grad = gelu_back(
+        affine_two, jnp.dot(branch_grad, point_full, preferred_element_type=jnp.float32)
+    )
     two_back = everywhere(
         jnp.stack([jnp.sum(affine_two_grad * normed_two, 0), jnp.sum(affine_two_grad, 0)])
     )
@@ -216,37 +465,31 @@
         )
     dilated_grad = jnp.stack(tap_grads)
     affine_one_grad = gelu_back(affine_one, hidden_one_grad)
-    one_back = everywhere(
-        jnp.stack([jnp.sum(affine_one_grad * normed_one, 0), jnp.sum(affine_one_grad, 0)])
-    )
-    input_grad = residual_grad + gain_one * inverse_one * (
-        affine_one_grad - one_back[1] / total_rows - normed_one * one_back[0] / total_rows
-    )
-    norm_full = jnp.concatenate([one_back[0], one_back[1], two_back[0], two_back[1]])
-    shard_len = norm_params.shape[0]
-    norm_grad = lax.dynamic_slice_in_dim(
-        norm_full, lax.axis_index(("seq", "trk")) * shard_len, shard_len
-    )
-    norm_momentum, norm_variance, norm_direction = moments(norm_first, norm_second, norm_grad)
-    norm_updated = norm_params - norm_rate * norm_direction
-    flat_grads = jnp.concatenate(
+    one_local = jnp.concatenate(
+        [jnp.sum(affine_one_grad * normed_one, 0), jnp.sum(affine_one_grad, 0)]
+    )
+    final_grad = final_grad.astype(low)
+    trunk_grads = jnp.concatenate(
         [
-            dilated_grad.astype(low).reshape(3, devices, -1).transpose(1, 0, 2).reshape(devices, -1),
-            point_grad.astype(low).T.reshape(devices, -1),
-            final_grad.astype(low).T.reshape(devices, -1),
+            dilated_grad.astype(low).reshape(3, devices, own, B).transpose(1, 0, 2, 3).reshape(devices, -1, B),
+            point_grad.astype(low).reshape(devices, own, B),
+            final_grad[:, :B].reshape(devices, -1, B),
+            final_grad[:, B:].reshape(devices, -1, B),
         ],
         1,
     )
-    flat_sum = lax.psum_scatter(
-        flat_grads.reshape(devices, -1, 128), ("seq", "trk"), scatter_dimension=0, tiled=True
-    ).reshape(-1)
-    flat_sum = flat_sum.astype(jnp.float32)
-    dilated_sum = flat_sum[: ends[0]].reshape(dilated_weight.shape)
-    point_sum = flat_sum[ends[0] : ends[1]].reshape(point_weight.shape[::-1]).T
-    final_sum = flat_sum[ends[1] : ends[2]].reshape(final_weight.shape[::-1]).T
-    head_sum = head_sum.astype(jnp.float32)
-    human_sum = head_sum[:, :human_cols]
-    mouse_sum = head_sum[:, human_pad:]
+    trunk_near = scattered_near(trunk_grads)
+    higher = digits(seq_count)[1:]
+    early_total = summed_digits(early_total, higher).astype(low)
+    late_total = summed_digits(after(late_total, trunk_near), higher).astype(low)
+    trunk_sum = scattered_far(trunk_near)
+    head_early = own_rows(early_total)
+    head_late = own_rows(late_total)
+    dilated_sum = trunk_sum[: 3 * own].reshape(3, own, B)
+    point_sum = trunk_sum[3 * own : 4 * own].T
+    final_sum = jnp.concatenate([trunk_sum[4 * own : 6 * own], trunk_sum[6 * own :]], 1).T
+    human_sum = jnp.concatenate(head_early + [head_late[0]], 1)[:, :human_cols]
+    mouse_sum = head_late[1][:, :mouse_cols]
     matrices = [
         (dilated_weight, dilated_first, dilated_second, dilated_sum),
         (point_weight, point_first, point_second, point_sum),
@@ -263,7 +506,23 @@
         results.append((momentum, variance, update, kernel_weight))
         weight_squares.append(jnp.sum(kernel_weight * kernel_weight))
         update_squares.append(jnp.sum(update * update))
-    square_sums = everywhere(jnp.stack([jnp.stack(weight_squares), jnp.stack(update_squares)]))
+    places = jnp.arange(128)
+    squares = jnp.zeros((128,), jnp.float32)
+    for index, square in enumerate(weight_squares + update_squares):
+        squares = jnp.where(places == index, square, squares)
+    last_sums = everywhere(jnp.concatenate([one_local, squares]))
+    one_back = last_sums[: 2 * C].reshape(2, C)
+    square_sums = last_sums[2 * C : 2 * C + 10].reshape(2, 5)
+    input_grad = residual_grad + gain_one * inverse_one * (
+        affine_one_grad - one_back[1] / total_rows - normed_one * one_back[0] / total_rows
+    )
+    norm_full = jnp.concatenate([one_back[0], one_back[1], two_back[0], two_back[1]])
+    shard_len = norm_params.shape[0]
+    norm_grad = lax.dynamic_slice_in_dim(
+        norm_full, lax.axis_index(("seq", "trk")) * shard_len, shard_len
+    )
+    norm_momentum, norm_variance, norm_direction = moments(norm_first, norm_second, norm_grad)
+    norm_updated = norm_params - norm_rate * norm_direction
     weight_norm = jnp.sqrt(square_sums[0])
     update_norm = jnp.sqrt(square_sums[1])
     ratio = weight_norm / (update_norm + adam_eps)

time: 688 us -> 463 us (0.67)
  waiting for transfers between devices: 471 us -> 228 us
  matrix products: 70.7 us -> 18 us
  starting transfers between devices: 36.4 us -> 87.6 us
  other arithmetic: 38 us -> 55.5 us
  local copies, waits for them, and re-layouts: 47.4 us -> 35.9 us
  Pallas kernels: 0 us -> 11.3 us
    reduce_scatter x2 -> x0, waiting for transfers between devices: 288 us -> none  [the longest x1 221 us: body(): lax.psum_scatter(contracted_rows(columns, joint_slope).astype(low), ('seq...]
    ppermute x0 -> x45, waiting for transfers between devices: none -> 144 us  [partner(): lax.ppermute(cells, axis, [(i, i ^ mask) for i in range(lax.axis_size(axi...]
    all_gather x1, waiting for transfers between devices: 105 us -> 23.7 us  [body(): heads = lax.all_gather(heads, ('seq', 'trk'), axis=0, tiled=True)]
    ppermute x0 -> x45, starting transfers between devices: none -> 54.1 us  [partner(): lax.ppermute(cells, axis, [(i, i ^ mask) for i in range(lax.axis_size(axi...]
    all_gather x1 -> x0, waiting for transfers between devices: 47.8 us -> none  [body(): trunk = lax.all_gather(flat.reshape(-1, 128), ('seq', 'trk'), axis=0)]
    all_to_all x5 -> x4, waiting for transfers between devices: 26.6 us -> 55.7 us  [everywhere(): return jnp.sum(lax.all_to_all(spread, axes, 0, 0, tiled=True), 0)]
    dot_general x4 -> x10, matrix products: 28.7 us -> 9.48 us  [the longest x8 7.34 us: product(): lax.dot_general(left, right, (((1,), (1,)), ((), ())), preferred_element_...]
    dot_general x7 -> x5, matrix products: 21.2 us -> 4.82 us  [contract_cols(): lax.dot_general(left, right, (((1,), (1,)), ((), ())), preferred_element_...]
  transfers between devices with their start and end apart: 13 -> 54, of which waited for: 10 -> 26; matrix products, arithmetic and copies ran while one was open for 8% -> 16% of each run, Pallas kernels for 0% -> 2%
where the time goes in v2:
time: 463 us; the launch traced here: 457 us
  waiting for transfers between devices  228 us (49%)
  starting transfers between devices  87.6 us (19%)
  other arithmetic  55.5 us (12%)
  local copies, waits for them, and re-layouts  35.9 us (8%)
  between operations  20.9 us (5%)
  matrix products  18 us (4%)
  Pallas kernels  11.3 us (2%)
    ppermute x45, waiting for transfers between devices, partner(): lax.ppermute(cells, axis, [(i, i ^ mask) for i in range(lax.axis_size(axi...  144 us
    all_to_all x4, waiting for transfers between devices, everywhere(): return jnp.sum(lax.all_to_all(spread, axes, 0, 0, tiled=True), 0)  55.7 us
    ppermute x45, starting transfers between devices, partner(): lax.ppermute(cells, axis, [(i, i ^ mask) for i in range(lax.axis_size(axi...  54.1 us
    all_to_all x4, starting transfers between devices, everywhere(): return jnp.sum(lax.all_to_all(spread, axes, 0, 0, tiled=True), 0)  26.1 us
    all_gather x1, waiting for transfers between devices, body(): heads = lax.all_gather(heads, ('seq', 'trk'), axis=0, tiled=True)  23.7 us
    pallas_call x1, Pallas kernels, heads_part(): pl.pallas_call(functools.partial(head_kernel, human_cols), grid_spec=pltp...  11.3 us
  transfers between devices with their start and end apart: 54, of which 26 were waited for; matrix products, arithmetic and copies ran while one was open for 16% of the time, Pallas kernels for 2%

profile of v2, /device:TPU:0, one launch (start us, length us, event | category | flops | bytes accessed | tf_op | source)
XLA Modules:
  0.0 456.8 jit_solution(8563856972520353551)
XLA Ops:
  10.6 5.1 %collective-permute-start = (bf16[1,80,384]{2,1,0:T(8,128)(2,1)S(1)}, bf16[1,80,384]{2,1,0:T(8,128)(2,1)S(1)}, u32[]{:S(2)}, u32[]{:S(2)}) collective-permute-start(bf16[1,80,384]{2,1,0:T(8,128)(2,1)S(1)} %maximum_bitcast_fusion.12), channel_id=1, source_target_pairs={{0,24},{4,28},{8,16},{12,20},{16,8},{20,12},{24,0},{28,4},{1,25},{... | collective-permute-start | bytes 184328 | tf_op jit(solution)/shard_map/ppermute | solution.py:68
  17.9 2.4 collective-permute-start.8
  26.2 8.9 %collective-permute-done.9 = bf16[1,120,384]{2,1,0:T(8,128)(2,1)S(1)} collective-permute-done((bf16[1,120,384]{2,1,0:T(8,128)(2,1)S(1)}, bf16[1,120,384]{2,1,0:T(8,128)(2,1)S(1)}, u32[]{:S(2)}, u32[]{:S(2)}) %collective-permute-start.9) | collective-permute-done | bytes 92192 | tf_op jit(solution)/shard_map/ppermute | solution.py:68
  38.8 4.1 collective-permute-done.11
  44.7 6.5 %collective-permute-done.4 = bf16[8,80,384]{2,1,0:T(8,128)(2,1)S(1)} collective-permute-done((bf16[8,80,384]{2,1,0:T(8,128)(2,1)S(1)}, bf16[8,80,384]{2,1,0:T(8,128)(2,1)S(1)}, u32[]{:S(2)}, u32[]{:S(2)}) %collective-permute-start.4) | collective-permute-done | bytes 491552 | tf_op jit(solution)/shard_map/ppermute | solution.py:68
  52.4 5.7 %all-to-all-start = ((f32[32,2,768]{2,1,0:T(2,128)}), f32[32,2,768]{2,1,0:T(2,128)S(1)}, u32[]{:S(2)}, u32[]{:S(2)}) async-start(f32[32,2,768]{2,1,0:T(2,128)} %broadcast_in_dim.77), calls=%async_computation | async-start | bytes 393216 | tf_op jit(solution)/shard_map/all_to_all | solution.py:64
  58.2 21.2 %all-to-all-done = f32[32,2,768]{2,1,0:T(2,128)S(1)} async-done(((f32[32,2,768]{2,1,0:T(2,128)}), f32[32,2,768]{2,1,0:T(2,128)S(1)}, u32[]{:S(2)}, u32[]{:S(2)}) %all-to-all-start) | async-done | bytes 196640 | tf_op jit(solution)/shard_map/all_to_all | solution.py:64
  84.3 2.4 collective-permute-start.6
  88.2 3.5 collective-permute-done.7
  93.8 6.2 %all-to-all-start.1 = ((f32[32,2,384]{2,1,0:T(2,128)}), f32[32,2,384]{2,1,0:T(2,128)S(1)}, u32[]{:S(2)}, u32[]{:S(2)}) async-start(f32[32,2,384]{2,1,0:T(2,128)} %broadcast_in_dim.79), calls=%async_computation.1 | async-start | bytes 196608 | tf_op jit(solution)/shard_map/all_to_all | solution.py:64
  100.0 10.6 %all-to-all-done.1 = f32[32,2,384]{2,1,0:T(2,128)S(1)} async-done(((f32[32,2,384]{2,1,0:T(2,128)}), f32[32,2,384]{2,1,0:T(2,128)S(1)}, u32[]{:S(2)}, u32[]{:S(2)}) %all-to-all-start.1) | async-done | bytes 98336 | tf_op jit(solution)/shard_map/all_to_all | solution.py:64
  122.6 34.3 %collective-permute-done.16 = bf16[1536,256]{1,0:T(8,128)(2,1)} collective-permute-done((bf16[1536,256]{1,0:T(8,128)(2,1)}, bf16[1536,256]{1,0:T(8,128)(2,1)}, u32[]{:S(2)}, u32[]{:S(2)}) %collective-permute-start.16) | collective-permute-done | bytes 786464 | tf_op jit(solution)/shard_map/ppermute | solution.py:68
  159.5 3.4 pad_maximum_fusion.2
  162.9 23.7 %all-gather.2.cloned.1.call-done.weights = bf16[1536,7168]{1,0:T(8,128)(2,1)} async-done(((bf16[48,7168]{1,0:T(8,128)(2,1)}), bf16[1536,7168]{1,0:T(8,128)(2,1)}) %all-gather.2.cloned.1.call-update) | async-done | bytes 22020112 | tf_op jit(solution)/shard_map/all_gather | solution.py:372
  187.8 11.3 %shard_map.381 = (f32[5313,256]{1,0:T(8,128)}, f32[1643,256]{1,0:T(8,128)}, bf16[7168,256]{1,0:T(8,128)(2,1)}, f32[1536,256]{1,0:T(8,128)S(1)}) custom-call(s32[1]{0:T(128)S(6)} %convert_element_type.235.flag, bf16[256,1536]{1,0:T(8,128)(2,1)S(1)} %get-tuple-element.180.features, bf16[1536,7168]{1,0:T(8,128)(2,1)} %all-gather.2.cloned.1.call-done.weights, ...), custom_call_target="tpu_custom_call" | custom-call | tf_op jit(solution)/shard_map/pallas_call | solution.py:285
  211.5 5.2 %collective-permute-start.20 = (bf16[2,2,448,256]{3,2,1,0:T(8,128)(2,1)}, bf16[2,2,448,256]{3,2,1,0:T(8,128)(2,1)}, u32[]{:S(2)}, u32[]{:S(2)}) collective-permute-start(bf16[2,2,448,256]{3,2,1,0:T(8,128)(2,1)} %pad_maximum_fusion.16), channel_id=1, source_target_pairs={{0,4},{4,0},{8,12},{12,8},{16,20},{20,16},{24,28},{28,24},{1,5},{5... | collective-permute-start | bytes 2752520 | tf_op jit(solution)/shard_map/ppermute | solution.py:68
  218.9 3.3 all-to-all-start.2
  224.1 14.5 %all-to-all-done.2 = f32[32,2,384]{2,1,0:T(2,128)} async-done(((f32[32,2,384]{2,1,0:T(2,128)}), f32[32,2,384]{2,1,0:T(2,128)}, u32[]{:S(2)}, u32[]{:S(2)}) %all-to-all-start.2) | async-done | bytes 98336 | tf_op jit(solution)/shard_map/all_to_all | solution.py:64
  253.9 2.8 collective-permute-start.21
  257.6 2.4 fusion.76
  268.8 8.4 %collective-permute-done.28 = bf16[4,2,96,384]{3,2,0,1:T(8,128)(2,1)S(1)} collective-permute-done((bf16[4,2,96,384]{3,2,0,1:T(8,128)(2,1)S(1)}, bf16[4,2,96,384]{3,2,0,1:T(8,128)(2,1)S(1)}, u32[]{:S(2)}, u32[]{:S(2)}) %collective-permute-start.28) | collective-permute-done | bytes 589856 | tf_op jit(solution)/shard_map/ppermute | solution.py:68
  284.1 3.2 collective-permute-done.29
  292.2 9.9 %collective-permute-done.22 = bf16[768,448]{0,1:T(8,128)(2,1)S(1)} collective-permute-done((bf16[768,448]{0,1:T(8,128)(2,1)S(1)}, bf16[768,448]{0,1:T(8,128)(2,1)S(1)}, u32[]{:S(2)}, u32[]{:S(2)}) %collective-permute-start.22) | collective-permute-done | bytes 688160 | tf_op jit(solution)/shard_map/ppermute | solution.py:68
  306.8 10.7 %collective-permute-done.37 = bf16[768,448]{0,1:T(8,128)(2,1)S(1)} collective-permute-done((bf16[768,448]{0,1:T(8,128)(2,1)S(1)}, bf16[768,448]{0,1:T(8,128)(2,1)S(1)}, u32[]{:S(2)}, u32[]{:S(2)}) %collective-permute-start.37) | collective-permute-done | bytes 688160 | tf_op jit(solution)/shard_map/ppermute | solution.py:68
  323.2 2.5 collective-permute-start.32
  331.9 8.8 %collective-permute-done.30 = bf16[192,896]{0,1:T(8,128)(2,1)S(1)} collective-permute-done((bf16[192,896]{0,1:T(8,128)(2,1)S(1)}, bf16[192,896]{0,1:T(8,128)(2,1)S(1)}, u32[]{:S(2)}, u32[]{:S(2)}) %collective-permute-start.30) | collective-permute-done | bytes 344096 | tf_op jit(solution)/shard_map/ppermute | solution.py:68
  340.7 11.9 %collective-permute-done.31 = bf16[192,896]{0,1:T(8,128)(2,1)S(1)} collective-permute-done((bf16[192,896]{0,1:T(8,128)(2,1)S(1)}, bf16[192,896]{0,1:T(8,128)(2,1)S(1)}, u32[]{:S(2)}, u32[]{:S(2)}) %collective-permute-start.31) | collective-permute-done | bytes 344096 | tf_op jit(solution)/shard_map/ppermute | solution.py:68
  359.5 32.4 %collective-permute-done.39 = bf16[192,896]{0,1:T(8,128)(2,1)} collective-permute-done((bf16[192,896]{0,1:T(8,128)(2,1)}, bf16[192,896]{0,1:T(8,128)(2,1)}, u32[]{:S(2)}, u32[]{:S(2)}) %collective-permute-start.39) | collective-permute-done | bytes 344096 | tf_op jit(solution)/shard_map/ppermute | solution.py:68
  405.7 3.1 multiply_reduce_fusion.1
  408.8 6.4 %compare_select_fusion.9 = f32[128]{0:T(128)S(1)} fusion(f32[]{:T(128)} %get-tuple-element.45, f32[]{:T(128)} %get-tuple-element.47, f32[]{:T(128)} %get-tuple-element.43, f32[]{:T(128)} %get-tuple-element.31, f32[]{:T(128)} %get-tuple-element.41, f32[]{:T(128)} %get-tuple-element.44, f32[]{:T(128)} %get-tuple-element.46, f32[]{:T(128)} %get-tuple-element.42, ...), kind=kLoop, calls=%fused_computation.402 | loop fusion | flops 2560 | bytes 552 | tf_op jit(solution)/shard_map/jit(_where)/select_n | solution.py:512
  416.1 11.0 %all-to-all-start.3 = ((f32[32,1,1664]{2,1,0:T(1,128)}), f32[32,1,1664]{2,1,0:T(1,128)}, u32[]{:S(2)}, u32[]{:S(2)}) async-start(f32[32,1,1664]{2,1,0:T(1,128)} %broadcast_in_dim.93), calls=%async_computation.3 | async-start | bytes 425984 | tf_op jit(solution)/shard_map/all_to_all | solution.py:64
  427.1 9.4 %all-to-all-done.3 = f32[32,1,1664]{2,1,0:T(1,128)} async-done(((f32[32,1,1664]{2,1,0:T(1,128)}), f32[32,1,1664]{2,1,0:T(1,128)}, u32[]{:S(2)}, u32[]{:S(2)}) %all-to-all-start.3) | async-done | bytes 213024 | tf_op jit(solution)/shard_map/all_to_all | solution.py:64
  (459 shorter events, 140.5 us)
Async XLA Ops:
  7.2 179.4 %all-gather.2.cloned.1.call-start = ((), (), s32[]{:S(2)}) async-start(), calls=%async_computation.4 | async-start | bytes 22708224 | tf_op jit(solution)/shard_map/all_gather | solution.py:372
  43.1 36.4 %collective-permute-start.12 = (bf16[8,120,384]{2,1,0:T(8,128)(2,1)S(1)}, bf16[8,120,384]{2,1,0:T(8,128)(2,1)}, u32[]{:S(2)}, u32[]{:S(2)}) collective-permute-start(bf16[8,120,384]{2,1,0:T(8,128)(2,1)S(1)} %bitcast.423), channel_id=1, source_target_pairs={{0,2},{1,3},{2,0},{3,1},{4,6},{5,7},{6,4},{7,5},{8,10},{9,11},{10,... | collective-permute-start | bytes 2211848 | tf_op jit(solution)/shard_map/ppermute | solution.py:68
  51.6 29.6 %collective-permute-start.5 = (bf16[16,80,384]{2,1,0:T(8,128)(2,1)S(1)}, bf16[16,80,384]{2,1,0:T(8,128)(2,1)S(1)}, u32[]{:S(2)}, u32[]{:S(2)}) collective-permute-start(bf16[16,80,384]{2,1,0:T(8,128)(2,1)S(1)} %bitcast.421), channel_id=1, source_target_pairs={{0,1},{1,0},{2,3},{3,2},{4,5},{5,4},{6,7},{7,6},{8,9},{9,8},{10,11... | collective-permute-start | bytes 2949128 | tf_op jit(solution)/shard_map/ppermute | solution.py:68
  52.4 27.0 %all-to-all-start = ((f32[32,2,768]{2,1,0:T(2,128)}), f32[32,2,768]{2,1,0:T(2,128)S(1)}, u32[]{:S(2)}, u32[]{:S(2)}) async-start(f32[32,2,768]{2,1,0:T(2,128)} %broadcast_in_dim.77), calls=%async_computation | async-start | bytes 393216 | tf_op jit(solution)/shard_map/all_to_all | solution.py:64
  81.1 30.2 %collective-permute-start.13 = (bf16[16,120,384]{2,1,0:T(8,128)(2,1)S(1)}, bf16[16,120,384]{2,1,0:T(8,128)(2,1)}, u32[]{:S(2)}, u32[]{:S(2)}) collective-permute-start(bf16[16,120,384]{2,1,0:T(8,128)(2,1)S(1)} %bitcast.416), channel_id=1, source_target_pairs={{0,1},{1,0},{2,3},{3,2},{4,5},{5,4},{6,7},{7,6},{8,9},{9,8},{10,11... | collective-permute-start | bytes 4423688 | tf_op jit(solution)/shard_map/ppermute | solution.py:68
  93.8 16.8 %all-to-all-start.1 = ((f32[32,2,384]{2,1,0:T(2,128)}), f32[32,2,384]{2,1,0:T(2,128)S(1)}, u32[]{:S(2)}, u32[]{:S(2)}) async-start(f32[32,2,384]{2,1,0:T(2,128)} %broadcast_in_dim.79), calls=%async_computation.1 | async-start | bytes 196608 | tf_op jit(solution)/shard_map/all_to_all | solution.py:64
  119.9 37.0 %collective-permute-start.16 = (bf16[1536,256]{1,0:T(8,128)(2,1)}, bf16[1536,256]{1,0:T(8,128)(2,1)}, u32[]{:S(2)}, u32[]{:S(2)}) collective-permute-start(bf16[1536,256]{1,0:T(8,128)(2,1)} %bitcast.55), channel_id=1, source_target_pairs={{0,2},{1,3},{2,0},{3,1},{4,6},{5,7},{6,4},{7,5},{8,10},{9,11},{10,... | collective-permute-start | bytes 2359304 | tf_op jit(solution)/shard_map/ppermute | solution.py:68
  121.7 37.1 %collective-permute-start.23 = (bf16[1536,256]{1,0:T(8,128)(2,1)}, bf16[1536,256]{1,0:T(8,128)(2,1)}, u32[]{:S(2)}, u32[]{:S(2)}) collective-permute-start(bf16[1536,256]{1,0:T(8,128)(2,1)} %bitcast.72), channel_id=1, source_target_pairs={{0,4},{4,0},{8,12},{12,8},{16,20},{20,16},{24,28},{28,24},{1,5},{5... | collective-permute-start | bytes 2359304 | tf_op jit(solution)/shard_map/ppermute | solution.py:68
  122.6 36.3 %collective-permute-start.17 = (bf16[1536,256]{1,0:T(8,128)(2,1)}, bf16[1536,256]{1,0:T(8,128)(2,1)}, u32[]{:S(2)}, u32[]{:S(2)}) collective-permute-start(bf16[1536,256]{1,0:T(8,128)(2,1)} %bitcast.55), channel_id=1, source_target_pairs={{0,1},{1,0},{2,3},{3,2},{4,5},{5,4},{6,7},{7,6},{8,9},{9,8},{10,11... | collective-permute-start | bytes 2359304 | tf_op jit(solution)/shard_map/ppermute | solution.py:68
  158.2 86.4 %collective-permute-start.24 = (bf16[1536,256]{1,0:T(8,128)(2,1)}, bf16[1536,256]{1,0:T(8,128)(2,1)}, u32[]{:S(2)}, u32[]{:S(2)}) collective-permute-start(bf16[1536,256]{1,0:T(8,128)(2,1)} %bitcast.72), channel_id=1, source_target_pairs={{0,1},{1,0},{2,3},{3,2},{4,5},{5,4},{6,7},{7,6},{8,9},{9,8},{10,11... | collective-permute-start | bytes 2359304 | tf_op jit(solution)/shard_map/ppermute | solution.py:68
  158.8 88.1 %collective-permute-start.25 = (bf16[1536,256]{1,0:T(8,128)(2,1)}, bf16[1536,256]{1,0:T(8,128)(2,1)}, u32[]{:S(2)}, u32[]{:S(2)}) collective-permute-start(bf16[1536,256]{1,0:T(8,128)(2,1)} %collective-permute-done.23), channel_id=1, source_target_pairs={{0,1},{1,0},{2,3},{3,2},{4,5},{5,4},{6,7},{7,6},{8,9},{9,8},{10,11... | collective-permute-start | bytes 2359304 | tf_op jit(solution)/shard_map/ppermute | solution.py:68
  209.1 41.9 %collective-permute-start.19 = (bf16[2,2,448,256]{3,2,1,0:T(8,128)(2,1)}, bf16[2,2,448,256]{3,2,1,0:T(8,128)(2,1)}, u32[]{:S(2)}, u32[]{:S(2)}) collective-permute-start(bf16[2,2,448,256]{3,2,1,0:T(8,128)(2,1)} %pad_maximum_fusion.15), channel_id=1, source_target_pairs={{0,2},{1,3},{2,0},{3,1},{4,6},{5,7},{6,4},{7,5},{8,10},{9,11},{10,... | collective-permute-start | bytes 2752520 | tf_op jit(solution)/shard_map/ppermute | solution.py:68
  211.5 40.8 %collective-permute-start.20 = (bf16[2,2,448,256]{3,2,1,0:T(8,128)(2,1)}, bf16[2,2,448,256]{3,2,1,0:T(8,128)(2,1)}, u32[]{:S(2)}, u32[]{:S(2)}) collective-permute-start(bf16[2,2,448,256]{3,2,1,0:T(8,128)(2,1)} %pad_maximum_fusion.16), channel_id=1, source_target_pairs={{0,4},{4,0},{8,12},{12,8},{16,20},{20,16},{24,28},{28,24},{1,5},{5... | collective-permute-start | bytes 2752520 | tf_op jit(solution)/shard_map/ppermute | solution.py:68
  218.9 19.8 %all-to-all-start.2 = ((f32[32,2,384]{2,1,0:T(2,128)}), f32[32,2,384]{2,1,0:T(2,128)}, u32[]{:S(2)}, u32[]{:S(2)}) async-start(f32[32,2,384]{2,1,0:T(2,128)} %broadcast_in_dim.81), calls=%async_computation.2 | async-start | bytes 196608 | tf_op jit(solution)/shard_map/all_to_all | solution.py:64
  261.1 16.1 %collective-permute-start.28 = (bf16[4,2,96,384]{3,2,0,1:T(8,128)(2,1)S(1)}, bf16[4,2,96,384]{3,2,0,1:T(8,128)(2,1)S(1)}, u32[]{:S(2)}, u32[]{:S(2)}) collective-permute-start(bf16[4,2,96,384]{3,2,0,1:T(8,128)(2,1)S(1)} %fusion.83), channel_id=1, source_target_pairs={{0,2},{1,3},{2,0},{3,1},{4,6},{5,7},{6,4},{7,5},{8,10},{9,11},{10,... | collective-permute-start | bytes 1769480 | tf_op jit(solution)/shard_map/ppermute | solution.py:68
  262.4 16.8 %collective-permute-start.44 = (bf16[4,2,96,384]{3,2,1,0:T(8,128)(2,1)S(1)}, bf16[4,2,96,384]{3,2,1,0:T(8,128)(2,1)S(1)}, u32[]{:S(2)}, u32[]{:S(2)}) collective-permute-start(bf16[4,2,96,384]{3,2,1,0:T(8,128)(2,1)S(1)} %fusion.82), channel_id=1, source_target_pairs={{0,4},{4,0},{8,12},{12,8},{16,20},{20,16},{24,28},{28,24},{1,5},{5... | collective-permute-start | bytes 1769480 | tf_op jit(solution)/shard_map/ppermute | solution.py:68
  280.7 21.4 %collective-permute-start.22 = (bf16[768,448]{0,1:T(8,128)(2,1)S(1)}, bf16[768,448]{0,1:T(8,128)(2,1)S(1)}, u32[]{:S(2)}, u32[]{:S(2)}) collective-permute-start(bf16[768,448]{0,1:T(8,128)(2,1)S(1)} %fusion.35), channel_id=1, source_target_pairs={{0,4},{4,0},{8,12},{12,8},{16,20},{20,16},{24,28},{28,24},{1,5},{5... | collective-permute-start | bytes 2064392 | tf_op jit(solution)/shard_map/ppermute | solution.py:68
  282.1 22.2 %collective-permute-start.26 = (bf16[768,448]{0,1:T(8,128)(2,1)S(1)}, bf16[768,448]{0,1:T(8,128)(2,1)S(1)}, u32[]{:S(2)}, u32[]{:S(2)}) collective-permute-start(bf16[768,448]{0,1:T(8,128)(2,1)S(1)} %fusion.41), channel_id=1, source_target_pairs={{0,2},{1,3},{2,0},{3,1},{4,6},{5,7},{6,4},{7,5},{8,10},{9,11},{10,... | collective-permute-start | bytes 2064392 | tf_op jit(solution)/shard_map/ppermute | solution.py:68
  282.7 34.8 %collective-permute-start.37 = (bf16[768,448]{0,1:T(8,128)(2,1)S(1)}, bf16[768,448]{0,1:T(8,128)(2,1)S(1)}, u32[]{:S(2)}, u32[]{:S(2)}) collective-permute-start(bf16[768,448]{0,1:T(8,128)(2,1)S(1)} %fusion.44), channel_id=1, source_target_pairs={{0,2},{1,3},{2,0},{3,1},{4,6},{5,7},{6,4},{7,5},{8,10},{9,11},{10,... | collective-permute-start | bytes 2064392 | tf_op jit(solution)/shard_map/ppermute | solution.py:68
  287.3 31.1 %collective-permute-start.36 = (bf16[768,448]{0,1:T(8,128)(2,1)S(1)}, bf16[768,448]{0,1:T(8,128)(2,1)S(1)}, u32[]{:S(2)}, u32[]{:S(2)}) collective-permute-start(bf16[768,448]{0,1:T(8,128)(2,1)S(1)} %fusion.38), channel_id=1, source_target_pairs={{0,4},{4,0},{8,12},{12,8},{16,20},{20,16},{24,28},{28,24},{1,5},{5... | collective-permute-start | bytes 2064392 | tf_op jit(solution)/shard_map/ppermute | solution.py:68
  289.9 33.3 %collective-permute-start.47 = (bf16[192,384]{1,0:T(8,128)(2,1)S(1)}, bf16[192,384]{1,0:T(8,128)(2,1)S(1)}, u32[]{:S(2)}, u32[]{:S(2)}) collective-permute-start(bf16[192,384]{1,0:T(8,128)(2,1)S(1)} %get-tuple-element.108), channel_id=1, source_target_pairs={{0,16},{4,20},{8,24},{12,28},{16,0},{20,4},{24,8},{28,12},{1,17},{... | collective-permute-start | bytes 442376 | tf_op jit(solution)/shard_map/ppermute | solution.py:68
  302.1 23.7 %collective-permute-start.48 = (bf16[192,384]{1,0:T(8,128)(2,1)S(1)}, bf16[192,384]{1,0:T(8,128)(2,1)S(1)}, u32[]{:S(2)}, u32[]{:S(2)}) collective-permute-start(bf16[192,384]{1,0:T(8,128)(2,1)S(1)} %get-tuple-element.109), channel_id=1, source_target_pairs={{0,24},{4,28},{8,16},{12,20},{16,8},{20,12},{24,0},{28,4},{1,25},{... | collective-permute-start | bytes 442376 | tf_op jit(solution)/shard_map/ppermute | solution.py:68
  304.3 21.4 %collective-permute-start.46 = (bf16[192,384]{1,0:T(8,128)(2,1)S(1)}, bf16[192,384]{1,0:T(8,128)(2,1)S(1)}, u32[]{:S(2)}, u32[]{:S(2)}) collective-permute-start(bf16[192,384]{1,0:T(8,128)(2,1)S(1)} %get-tuple-element.70), channel_id=1, source_target_pairs={{0,8},{4,12},{8,0},{12,4},{16,24},{20,28},{24,16},{28,20},{1,9},{5... | collective-permute-start | bytes 442376 | tf_op jit(solution)/shard_map/ppermute | solution.py:68
  317.5 23.2 %collective-permute-start.30 = (bf16[192,896]{0,1:T(8,128)(2,1)S(1)}, bf16[192,896]{0,1:T(8,128)(2,1)S(1)}, u32[]{:S(2)}, u32[]{:S(2)}) collective-permute-start(bf16[192,896]{0,1:T(8,128)(2,1)S(1)} %get-tuple-element.105), channel_id=1, source_target_pairs={{0,8},{4,12},{8,0},{12,4},{16,24},{20,28},{24,16},{28,20},{1,9},{5... | collective-permute-start | bytes 1032200 | tf_op jit(solution)/shard_map/ppermute | solution.py:68
  318.4 34.1 %collective-permute-start.31 = (bf16[192,896]{0,1:T(8,128)(2,1)S(1)}, bf16[192,896]{0,1:T(8,128)(2,1)S(1)}, u32[]{:S(2)}, u32[]{:S(2)}) collective-permute-start(bf16[192,896]{0,1:T(8,128)(2,1)S(1)} %get-tuple-element.107), channel_id=1, source_target_pairs={{0,16},{4,20},{8,24},{12,28},{16,0},{20,4},{24,8},{28,12},{1,17},{... | collective-permute-start | bytes 1032200 | tf_op jit(solution)/shard_map/ppermute | solution.py:68
  323.2 29.3 %collective-permute-start.32 = (bf16[192,896]{0,1:T(8,128)(2,1)S(1)}, bf16[192,896]{0,1:T(8,128)(2,1)S(1)}, u32[]{:S(2)}, u32[]{:S(2)}) collective-permute-start(bf16[192,896]{0,1:T(8,128)(2,1)S(1)} %get-tuple-element.106), channel_id=1, source_target_pairs={{0,24},{4,28},{8,16},{12,20},{16,8},{20,12},{24,0},{28,4},{1,25},{... | collective-permute-start | bytes 1032200 | tf_op jit(solution)/shard_map/ppermute | solution.py:68
  325.8 33.8 %collective-permute-start.38 = (bf16[192,896]{0,1:T(8,128)(2,1)}, bf16[192,896]{0,1:T(8,128)(2,1)}, u32[]{:S(2)}, u32[]{:S(2)}) collective-permute-start(bf16[192,896]{0,1:T(8,128)(2,1)} %get-tuple-element.102), channel_id=1, source_target_pairs={{0,8},{4,12},{8,0},{12,4},{16,24},{20,28},{24,16},{28,20},{1,9},{5... | collective-permute-start | bytes 1032200 | tf_op jit(solution)/shard_map/ppermute | solution.py:68
  325.8 66.2 %collective-permute-start.39 = (bf16[192,896]{0,1:T(8,128)(2,1)}, bf16[192,896]{0,1:T(8,128)(2,1)}, u32[]{:S(2)}, u32[]{:S(2)}) collective-permute-start(bf16[192,896]{0,1:T(8,128)(2,1)} %get-tuple-element.104), channel_id=1, source_target_pairs={{0,16},{4,20},{8,24},{12,28},{16,0},{20,4},{24,8},{28,12},{1,17},{... | collective-permute-start | bytes 1032200 | tf_op jit(solution)/shard_map/ppermute | solution.py:68
  340.7 51.3 %collective-permute-start.40 = (bf16[192,896]{0,1:T(8,128)(2,1)}, bf16[192,896]{0,1:T(8,128)(2,1)}, u32[]{:S(2)}, u32[]{:S(2)}) collective-permute-start(bf16[192,896]{0,1:T(8,128)(2,1)} %get-tuple-element.103), channel_id=1, source_target_pairs={{0,24},{4,28},{8,16},{12,20},{16,8},{20,12},{24,0},{28,4},{1,25},{... | collective-permute-start | bytes 1032200 | tf_op jit(solution)/shard_map/ppermute | solution.py:68
  356.1 39.5 %collective-permute-start.34 = (bf16[2,48,448]{2,1,0:T(8,128)(2,1)S(1)}, bf16[2,48,448]{2,1,0:T(8,128)(2,1)}, u32[]{:S(2)}, u32[]{:S(2)}) collective-permute-start(bf16[2,48,448]{2,1,0:T(8,128)(2,1)S(1)} %dynamic-slice_bitcast_fusion.11), channel_id=1, source_target_pairs={{0,2},{1,3},{2,0},{3,1},{4,6},{5,7},{6,4},{7,5},{8,10},{9,11},{10,... | collective-permute-start | bytes 258056 | tf_op jit(solution)/shard_map/ppermute | solution.py:68
  358.1 38.5 %collective-permute-start.33 = (bf16[2,48,448]{2,1,0:T(8,128)(2,1)S(1)}, bf16[2,48,448]{2,1,0:T(8,128)(2,1)}, u32[]{:S(2)}, u32[]{:S(2)}) collective-permute-start(bf16[2,48,448]{2,1,0:T(8,128)(2,1)S(1)} %dynamic-slice_bitcast_fusion.12), channel_id=1, source_target_pairs={{0,4},{4,0},{8,12},{12,8},{16,20},{20,16},{24,28},{28,24},{1,5},{5... | collective-permute-start | bytes 258056 | tf_op jit(solution)/shard_map/ppermute | solution.py:68
  416.1 20.4 %all-to-all-start.3 = ((f32[32,1,1664]{2,1,0:T(1,128)}), f32[32,1,1664]{2,1,0:T(1,128)}, u32[]{:S(2)}, u32[]{:S(2)}) async-start(f32[32,1,1664]{2,1,0:T(1,128)} %broadcast_in_dim.93), calls=%async_computation.3 | async-start | bytes 425984 | tf_op jit(solution)/shard_map/all_to_all | solution.py:64
  (112 other events, 1030.8 us)
Sparse Core Ops, SparseCore 0:
  11.5 175.0 all-gather.1
